TPU v7x, 32 devices: a whole 2x2x4 slice. The times are simulated.
32 devices in a mesh: sx: 8 (over z, y), sy: 4 (over x, core).
Axes of the slice: x: 2, y: 2, z: 4, core: 2. Of those that a mesh axis runs over, the one named last changes fastest.
Arguments:
- rhs: float32 [6144, 8192], P('sx', 'sy')
- sigma: float32 [6144, 8192], P('sx', 'sy'), may hold values from 0.05 to 2
- tile_list: int32 [65536], P(('sx', 'sy')), may hold values from 0 to 12287, as said below
- tile_owner: int32 [65536, 1], P(('sx', 'sy')), may hold values from 0 to 31, as said below
- schur_blocks: bfloat16 [32, 128, 128], P(('sx', 'sy')), as said below
Outputs:
- corrected: float32 [6144, 8192], P('sx', 'sy')
- iface_residual: float32 [65536, 128], P(('sx', 'sy'))
- iface_direction: float32 [65536, 128], P(('sx', 'sy'))
Inputs may be any that keep to these rules, and one draw needn't show every extreme that they name: `tile_owner`: within the 2048 tiles of one subdomain no owner appears more than 128 times. `tile_list`: every listed run touches its block's rim: it lies in the block's first or last row, or is the first or last run of its row. Runs may repeat. `schur_blocks`: each block is symmetric.
All inputs are finite; a program needn't handle non-finite values.
Results may differ from a plain program's by a relative error of at most 0.012.
Values may be sent and summed in bfloat16 or wider, within the bound.
A program may use at most 128 MiB of HBM per device.

v0:
```python
import jax
import jax.numpy as jnp
from jax import lax
from jax.sharding import PartitionSpec as P


def padded_2(shard, sides, width):
    for axis, dim in sides:
        devices, length = (lax.axis_size(axis), shard.shape[dim])
        up = [(i, (i + 1) % devices) for i in range(devices - 1)]
        down = [(j, i) for i, j in up]
        last = lax.slice_in_dim(shard, length - width, length, axis=dim)
        initial = lax.slice_in_dim(shard, 0, width, axis=dim)
        before = lax.ppermute(last, axis, up)
        after = lax.ppermute(initial, axis, down)
        shard = jnp.concatenate([before, shard, after], axis=dim)
    return shard


def apply_op(field, sigma):
    padded = padded_2(field, (("sx", 0), ("sy", 1)), 1)
    beside = padded[2:, 1:-1] + padded[:-2, 1:-1] + padded[1:-1, 2:] + padded[1:-1, :-2]
    return (4.0 + sigma) * field - beside


def per_device(rhs, sigma, tile_list, tile_owner, schur_blocks):
    width = schur_blocks.shape[2]
    dinv = 1.0 / (4.0 + sigma)
    first = 0.6111111 * dinv * rhs
    second = first + 2.75 * dinv * (rhs - apply_op(first, sigma))
    field_res = rhs - apply_op(second, sigma)
    r_tiles = field_res.reshape(-1, width)[tile_list]
    p_half = r_tiles.astype(jnp.bfloat16)
    owner = tile_owner[:, 0]
    count_tiles = tile_list.shape[0]
    nsx = lax.axis_size("sx")
    nsy = lax.axis_size("sy")
    devices = nsx * nsy
    capacity = 2 * count_tiles // devices
    onehot = (owner[:, None] == jnp.arange(devices, dtype=jnp.int32)[None, :]).astype(jnp.int32)
    ranks = jnp.cumsum(onehot, axis=0) - onehot
    slot = jnp.sum(ranks * onehot, axis=1)
    target = owner * capacity + slot
    buffer = jnp.zeros((devices * capacity, width), jnp.bfloat16).at[target].set(p_half)
    own_block = schur_blocks[0]
    boxed = buffer.reshape(devices, capacity, width)
    boxes = lax.all_to_all(boxed, ("sx", "sy"), split_axis=0, concat_axis=0, tiled=True)
    flat = boxes.reshape(-1, width)
    prod = jnp.dot(flat, own_block, preferred_element_type=jnp.float32)
    products = prod.astype(jnp.bfloat16).reshape(boxes.shape)
    returned = lax.all_to_all(products, ("sx", "sy"), split_axis=0, concat_axis=0, tiled=True)
    q_tiles = returned.reshape(-1, width)[target].astype(jnp.float32)
    rr_old, pq_sum, qq_sum = lax.psum(
        (jnp.sum(r_tiles * r_tiles), jnp.sum(r_tiles * q_tiles), jnp.sum(q_tiles * q_tiles)),
        ("sx", "sy"),
    )
    alpha = rr_old / pq_sum
    iface_residual = r_tiles - alpha * q_tiles
    rr_new = rr_old - 2.0 * alpha * pq_sum + alpha * alpha * qq_sum
    iface_direction = iface_residual + rr_new / rr_old * r_tiles
    corrected = second.reshape(-1, width).at[tile_list].add(alpha * r_tiles).reshape(second.shape)
    return (corrected, iface_residual, iface_direction)


def solution(mesh):
    in_specs = (
        P("sx", "sy"),
        P("sx", "sy"),
        P(("sx", "sy")),
        P(("sx", "sy"), None),
        P(("sx", "sy"), None, None),
    )
    out_specs = (P("sx", "sy"), P(("sx", "sy"), None), P(("sx", "sy"), None))
    return jax.shard_map(
        per_device, mesh=mesh, in_specs=in_specs, out_specs=out_specs, check_vma=False
    )
```

profile of v0, /device:TPU:0, one launch (start us, length us, event | category | flops | bytes accessed | tf_op | source)
XLA Modules:
  0.0 243.7 jit_solution(6434073895313553003)
XLA Ops:
  0.6 0.0 copy-start
  0.7 6.0 %multiply_multiply_fusion = f32[768,2048]{1,0:T(8,128)S(1)} fusion(f32[768,2048]{1,0:T(8,128)} %param.5, f32[768,2048]{1,0:T(8,128)} %param.6), kind=kLoop, calls=%fused_computation.32 | loop fusion | flops 6291456 | bytes 18874368 | tf_op jit(solution)/shard_map/mul | solution.py:29
  6.6 0.0 copy-start.2
  6.6 2.7 %copy-done.2 = f32[768,2048]{1,0:T(8,128)} copy-done((f32[768,2048]{1,0:T(8,128)}, f32[768,2048]{1,0:T(8,128)S(1)}, u32[]{:S(2)}) %copy-start.2) | copy-done | bytes 6291480
  9.3 1.3 collective-permute-start
  10.6 5.5 %collective-permute-start.1 = (f32[1,2048]{1,0:T(1,128)S(1)}, f32[1,2048]{1,0:T(1,128)S(1)}, u32[]{:S(2)}, u32[]{:S(2)}) collective-permute-start(f32[1,2048]{1,0:T(1,128)S(1)} %get-tuple-element.17), channel_id=1, source_target_pairs={{0,4},{4,8},{8,12},{12,16},{16,20},{20,24},{24,28},{1,5},{5,9},{9,... | collective-permute-start | bytes 24584 | tf_op jit(solution)/shard_map/ppermute | solution.py:14
  16.2 9.1 %reduce-window.6 = s32[32,16,128]{2,1,0:T(8,128)S(1)} reduce-window(s32[32,16,128]{2,1,0:T(8,128)S(1)} %fusion.24, s32[]{:T(128)} %constant.5.clone.1), window={size=1x1x128 pad=0_0x0_0x127_0}, to_apply=%region_2.3 | reduce-window | flops 8323072 | bytes 524292 | tf_op jit(solution)/shard_map/reduce-window
  25.3 0.1 slice.88
  25.4 0.2 copy.10
  25.6 0.2 reduce-window.9
  25.8 0.1 broadcast_add_fusion
  26.0 0.0 collective-permute-done
  26.0 0.0 collective-permute-done.1
  26.0 1.4 pad_maximum_fusion.21
  27.5 1.4 collective-permute-start.2
  28.9 3.1 %collective-permute-start.3 = (f32[770,1]{1,0:T(8,128)S(1)}, f32[770,1]{1,0:T(8,128)S(1)}, u32[]{:S(2)}, u32[]{:S(2)}) collective-permute-start(f32[770,1]{1,0:T(8,128)S(1)} %get-tuple-element.14), channel_id=1, source_target_pairs={{0,1},{1,2},{2,3},{4,5},{5,6},{6,7},{8,9},{9,10},{10,11},{12,13},{... | collective-permute-start | bytes 9248 | tf_op jit(solution)/shard_map/ppermute | solution.py:14
  32.0 0.0 slice-start
  32.0 0.1 fusion.23
  32.1 0.0 slice-start.1
  32.1 0.0 collective-permute-done.2
  32.1 1.2 collective-permute-done.3
  33.3 12.7 %fusion.9 = f32[768,2048]{1,0:T(8,128)S(1)} fusion(f32[768,2048]{1,0:T(8,128)S(1)} %copy-done.3, f32[768,2048]{1,0:T(8,128)} %param.5, f32[770,1]{1,0:T(8,128)S(1)} %collective-permute-done.3, f32[1,2048]{1,0:T(1,128)S(1)} %collective-permute-done, f32[1,2048]{1,0:T(1,128)S(1)} %collective-permute-done.1, f32[770,1]{1,0:T(8,128)S(1)} %collective-permute-done.2, ...), kind=kLoop, calls=%fused_computation.22 | loop fusion | flops 29884416 | bytes 25188368 | tf_op jit(solution)/shard_map/add | solution.py:30
  46.0 0.0 copy-start.1
  46.0 0.0 copy-start.5
  46.0 1.3 collective-permute-start.4
  47.3 5.4 %collective-permute-start.5 = (f32[1,2048]{1,0:T(1,128)S(1)}, f32[1,2048]{1,0:T(1,128)S(1)}, u32[]{:S(2)}, u32[]{:S(2)}) collective-permute-start(f32[1,2048]{1,0:T(1,128)S(1)} %get-tuple-element.15), channel_id=1, source_target_pairs={{0,4},{4,8},{8,12},{12,16},{16,20},{20,24},{24,28},{1,5},{5,9},{9,... | collective-permute-start | bytes 24584 | tf_op jit(solution)/shard_map/ppermute | solution.py:14
  52.8 0.0 collective-permute-done.4
  52.8 1.3 collective-permute-done.5
  54.1 0.2 pad_maximum_fusion.18
  54.3 1.3 collective-permute-start.6
  55.6 5.7 %collective-permute-start.7 = (f32[770,1]{1,0:T(8,128)S(1)}, f32[770,1]{1,0:T(8,128)S(1)}, u32[]{:S(2)}, u32[]{:S(2)}) collective-permute-start(f32[770,1]{1,0:T(8,128)S(1)} %get-tuple-element.12), channel_id=1, source_target_pairs={{0,1},{1,2},{2,3},{4,5},{5,6},{6,7},{8,9},{9,10},{10,11},{12,13},{... | collective-permute-start | bytes 9248 | tf_op jit(solution)/shard_map/ppermute | solution.py:14
  61.3 0.0 collective-permute-done.6
  61.3 1.3 collective-permute-done.7
  62.6 12.7 %fusion.2 = f32[768,2048]{1,0:T(8,128)} fusion(f32[768,2048]{1,0:T(8,128)S(1)} %bitcast.33, f32[770,1]{1,0:T(8,128)S(1)} %collective-permute-done.7, f32[1,2048]{1,0:T(1,128)S(1)} %collective-permute-done.4, f32[768,2048]{1,0:T(8,128)S(1)} %fusion.9, f32[1,2048]{1,0:T(1,128)S(1)} %collective-permute-done.5, f32[770,1]{1,0:T(8,128)S(1)} %collective-permute-done.6, ...), kind=kLoop, calls=%fused_computation.7 | loop fusion | flops 23592960 | bytes 25188368 | tf_op jit(solution)/shard_map/sub | solution.py:31
  75.3 7.1 %reshape.45 = f32[12288,128]{1,0:T(8,128)} reshape(f32[768,2048]{1,0:T(8,128)} %fusion.2) | data formatting | bytes 12582912 | tf_op jit(solution)/shard_map/reshape | solution.py:32
  82.3 8.2 %gather_fusion = f32[2048,128]{1,0:T(8,128)S(1)} fusion(f32[12288,128]{1,0:T(8,128)} %reshape.45, s32[2048]{0:T(1024)S(1)} %get-tuple-element.19), kind=kCustom, calls=%fused_computation | custom fusion | bytes 2105344 | tf_op jit(solution)/shard_map/gather | solution.py:32
  90.6 6.0 %scatter_custom_fusion = bf16[4096,128]{1,0:T(8,128)(2,1)S(1)} fusion(s32[2048]{0:T(1024)S(1)} %bitcast.43, f32[2048,128]{1,0:T(8,128)S(1)} %gather_fusion, bf16[]{:T(256)} %constant.8.clone.1), kind=kCustom, calls=%fused_computation.46 | custom fusion | flops 262144 | bytes 2097154 | tf_op jit(solution)/shard_map/scatter | solution.py:44
  96.6 41.6 %all_to_all.10 = bf16[32,128,128]{2,1,0:T(8,128)(2,1)S(1)} all-to-all(bf16[32,128,128]{2,1,0:T(8,128)(2,1)S(1)} %bitcast.35), channel_id=1, replica_groups=mesh['sx'=8,'sy'=4] {'sx','sy'}, dimensions={0} | all-to-all | bytes 2097152 | tf_op jit(solution)/shard_map/all_to_all | solution.py:47
  138.3 1.4 convolution_convert_fusion
  139.7 3.8 %all-to-all-start.1 = ((bf16[32,128,128]{2,1,0:T(8,128)(2,1)}), bf16[32,128,128]{2,1,0:T(8,128)(2,1)S(1)}, u32[]{:S(2)}, u32[]{:S(2)}) async-start(bf16[32,128,128]{2,1,0:T(8,128)(2,1)} %bitcast.10), calls=%async_computation.1 | async-start | bytes 2097152 | tf_op jit(solution)/shard_map/all_to_all | solution.py:51
  143.5 7.1 %reshape.44 = f32[12288,128]{1,0:T(8,128)} reshape(f32[768,2048]{1,0:T(8,128)} %copy-done.1) | data formatting | bytes 12582912 | tf_op jit(solution)/shard_map/reshape | solution.py:61
  150.6 19.0 %all-to-all-done.1 = bf16[32,128,128]{2,1,0:T(8,128)(2,1)S(1)} async-done(((bf16[32,128,128]{2,1,0:T(8,128)(2,1)}), bf16[32,128,128]{2,1,0:T(8,128)(2,1)S(1)}, u32[]{:S(2)}, u32[]{:S(2)}) %all-to-all-start.1) | async-done | bytes 1048608 | tf_op jit(solution)/shard_map/all_to_all | solution.py:51
  169.5 6.2 %gather_fusion.1 = bf16[2048,128]{1,0:T(8,128)(2,1)S(1)} fusion(bf16[4096,128]{1,0:T(8,128)(2,1)S(1)} %bitcast.34, s32[2048]{0:T(1024)S(1)} %broadcast_clamp_fusion), kind=kCustom, calls=%fused_computation.1 | custom fusion | bytes 1056768 | tf_op jit(solution)/shard_map/gather | solution.py:52
  175.7 0.9 fusion.12
  176.6 38.8 %all-reduce = (f32[]{:T(128)}, f32[]{:T(128)}, f32[]{:T(128)}) all-reduce(f32[]{:T(128)} %get-tuple-element.4, f32[]{:T(128)} %get-tuple-element.3, f32[]{:T(128)} %get-tuple-element.5), channel_id=1, replica_groups=mesh['sx'=8,'sy'=4] {'sx','sy'}, use_global_device_ids=true, to_apply=%region_1.2 | all-reduce | flops 3 | bytes 24 | tf_op jit(solution)/shard_map/psum | solution.py:53
  219.3 1.5 multiply_add_fusion
  220.8 15.8 %scatter_custom_fusion.1 = f32[12288,128]{1,0:T(8,128)} fusion(f32[12288,128]{1,0:T(8,128)} %reshape.44, s32[2048]{0:T(1024)S(1)} %get-tuple-element.20, f32[2048,128]{1,0:T(8,128)S(1)} %gather_fusion, f32[]{:T(128)S(6)} %div.14), kind=kCustom, calls=%fused_computation.42 | custom fusion | flops 524288 | bytes 7340036 | tf_op jit(solution)/shard_map/scatter-add | solution.py:61
  236.6 7.1 %reshape.51 = f32[768,2048]{1,0:T(8,128)} reshape(f32[12288,128]{1,0:T(8,128)} %scatter_custom_fusion.1) | data formatting | bytes 12582912 | tf_op jit(solution)/shard_map/reshape | solution.py:61
  (16 shorter events, 0.1 us)
Async XLA Ops:
  0.6 137.6 %copy-start = (bf16[1,128,128]{2,1,0:T(8,128)(2,1)S(1)}, bf16[1,128,128]{2,1,0:T(8,128)(2,1)}, u32[]{:S(2)}) copy-start(bf16[1,128,128]{2,1,0:T(8,128)(2,1)} %param.9) | copy-start | bytes 98308
  0.6 15.5 %copy-start.4 = (s32[2048,1]{0,1:T(1,128)S(1)}, s32[2048,1]{0,1:T(1,128)}, u32[]{:S(2)}) copy-start(s32[2048,1]{0,1:T(1,128)} %param.8) | copy-start | bytes 24580
  6.6 2.7 %copy-start.2 = (f32[768,2048]{1,0:T(8,128)}, f32[768,2048]{1,0:T(8,128)S(1)}, u32[]{:S(2)}) copy-start(f32[768,2048]{1,0:T(8,128)S(1)} %multiply_multiply_fusion) | copy-start | bytes 18874372
  9.3 16.6 %collective-permute-start = (f32[1,2048]{1,0:T(1,128)S(1)}, f32[1,2048]{1,0:T(1,128)S(1)}, u32[]{:S(2)}, u32[]{:S(2)}) collective-permute-start(f32[1,2048]{1,0:T(1,128)S(1)} %get-tuple-element.18), channel_id=1, source_target_pairs={{4,0},{8,4},{12,8},{16,12},{20,16},{24,20},{28,24},{5,1},{9,5},{13... | collective-permute-start | bytes 24584 | tf_op jit(solution)/shard_map/ppermute | solution.py:15
  10.6 15.4 %collective-permute-start.1 = (f32[1,2048]{1,0:T(1,128)S(1)}, f32[1,2048]{1,0:T(1,128)S(1)}, u32[]{:S(2)}, u32[]{:S(2)}) collective-permute-start(f32[1,2048]{1,0:T(1,128)S(1)} %get-tuple-element.17), channel_id=1, source_target_pairs={{0,4},{4,8},{8,12},{12,16},{16,20},{20,24},{24,28},{1,5},{5,9},{9,... | collective-permute-start | bytes 24584 | tf_op jit(solution)/shard_map/ppermute | solution.py:14
  25.8 7.4 %copy-start.3 = (f32[768,2048]{1,0:T(8,128)S(1)}, f32[768,2048]{1,0:T(8,128)}, u32[]{:S(2)}) copy-start(f32[768,2048]{1,0:T(8,128)} %copy-done.2) | copy-start | bytes 18874372
  27.5 4.6 %collective-permute-start.2 = (f32[770,1]{1,0:T(8,128)S(1)}, f32[770,1]{1,0:T(8,128)S(1)}, u32[]{:S(2)}, u32[]{:S(2)}) collective-permute-start(f32[770,1]{1,0:T(8,128)S(1)} %get-tuple-element.13), channel_id=1, source_target_pairs={{1,0},{2,1},{3,2},{5,4},{6,5},{7,6},{9,8},{10,9},{11,10},{13,12},{... | collective-permute-start | bytes 9248 | tf_op jit(solution)/shard_map/ppermute | solution.py:15
  28.9 4.4 %collective-permute-start.3 = (f32[770,1]{1,0:T(8,128)S(1)}, f32[770,1]{1,0:T(8,128)S(1)}, u32[]{:S(2)}, u32[]{:S(2)}) collective-permute-start(f32[770,1]{1,0:T(8,128)S(1)} %get-tuple-element.14), channel_id=1, source_target_pairs={{0,1},{1,2},{2,3},{4,5},{5,6},{6,7},{8,9},{9,10},{10,11},{12,13},{... | collective-permute-start | bytes 9248 | tf_op jit(solution)/shard_map/ppermute | solution.py:14
  32.0 30.6 %slice-start = ((s8[6291456]{0:T(1024)(128)(4,1)}), s8[4194304]{0:T(1024)(128)(4,1)S(1)}, s32[]{:S(2)}) async-start(s8[6291456]{0:T(1024)(128)(4,1)} %bitcast.32), calls=%async_computation.2 | async-start | bytes 8388608
  32.1 30.5 %slice-start.1 = ((s8[6291456]{0:T(1024)(128)(4,1)}), s8[2097152]{0:T(1024)(128)(4,1)S(1)}, s32[]{:S(2)}) async-start(s8[6291456]{0:T(1024)(128)(4,1)} %bitcast.32), calls=%async_computation.3 | async-start | bytes 4194304
  46.0 16.6 %copy-start.1 = (f32[768,2048]{1,0:T(8,128)}, f32[768,2048]{1,0:T(8,128)S(1)}, u32[]{:S(2)}) copy-start(f32[768,2048]{1,0:T(8,128)S(1)} %fusion.9) | copy-start | bytes 18874372
  46.0 15.3 %copy-start.5 = (s32[2048]{0:T(1024)S(1)}, s32[2048]{0:T(1024)}, u32[]{:S(2)}) copy-start(s32[2048]{0:T(1024)} %param.7) | copy-start | bytes 24580
  46.0 6.8 %collective-permute-start.4 = (f32[1,2048]{1,0:T(1,128)S(1)}, f32[1,2048]{1,0:T(1,128)S(1)}, u32[]{:S(2)}, u32[]{:S(2)}) collective-permute-start(f32[1,2048]{1,0:T(1,128)S(1)} %get-tuple-element.16), channel_id=1, source_target_pairs={{4,0},{8,4},{12,8},{16,12},{20,16},{24,20},{28,24},{5,1},{9,5},{13... | collective-permute-start | bytes 24584 | tf_op jit(solution)/shard_map/ppermute | solution.py:15
  47.3 6.8 %collective-permute-start.5 = (f32[1,2048]{1,0:T(1,128)S(1)}, f32[1,2048]{1,0:T(1,128)S(1)}, u32[]{:S(2)}, u32[]{:S(2)}) collective-permute-start(f32[1,2048]{1,0:T(1,128)S(1)} %get-tuple-element.15), channel_id=1, source_target_pairs={{0,4},{4,8},{8,12},{12,16},{16,20},{20,24},{24,28},{1,5},{5,9},{9,... | collective-permute-start | bytes 24584 | tf_op jit(solution)/shard_map/ppermute | solution.py:14
  54.3 7.0 %collective-permute-start.6 = (f32[770,1]{1,0:T(8,128)S(1)}, f32[770,1]{1,0:T(8,128)S(1)}, u32[]{:S(2)}, u32[]{:S(2)}) collective-permute-start(f32[770,1]{1,0:T(8,128)S(1)} %get-tuple-element.11), channel_id=1, source_target_pairs={{1,0},{2,1},{3,2},{5,4},{6,5},{7,6},{9,8},{10,9},{11,10},{13,12},{... | collective-permute-start | bytes 9248 | tf_op jit(solution)/shard_map/ppermute | solution.py:15
  55.6 7.0 %collective-permute-start.7 = (f32[770,1]{1,0:T(8,128)S(1)}, f32[770,1]{1,0:T(8,128)S(1)}, u32[]{:S(2)}, u32[]{:S(2)}) collective-permute-start(f32[770,1]{1,0:T(8,128)S(1)} %get-tuple-element.12), channel_id=1, source_target_pairs={{0,1},{1,2},{2,3},{4,5},{5,6},{6,7},{8,9},{9,10},{10,11},{12,13},{... | collective-permute-start | bytes 9248 | tf_op jit(solution)/shard_map/ppermute | solution.py:14
  139.7 29.9 %all-to-all-start.1 = ((bf16[32,128,128]{2,1,0:T(8,128)(2,1)}), bf16[32,128,128]{2,1,0:T(8,128)(2,1)S(1)}, u32[]{:S(2)}, u32[]{:S(2)}) async-start(bf16[32,128,128]{2,1,0:T(8,128)(2,1)} %bitcast.10), calls=%async_computation.1 | async-start | bytes 2097152 | tf_op jit(solution)/shard_map/all_to_all | solution.py:51
where the time goes:
time: 245 us; the launch traced here: 244 us
  blocking collectives  80.4 us (33%)
  other arithmetic  66.8 us (27%)
  local copies, waits for them, and re-layouts  38.8 us (16%)
  starting transfers between devices  28.8 us (12%)
  waiting for transfers between devices  22.7 us (9%)
  between operations  4.9 us (2%)
    all_to_all x1, blocking collectives, per_device(): lax.all_to_all(boxed, ('sx', 'sy'), split_axis=0, concat_axis=0, tiled=True)  41.6 us
    psum x1, blocking collectives, per_device(): lax.psum((jnp.sum(r_tiles * r_tiles), jnp.sum(r_tiles * q_tiles), jnp.sum...  38.8 us
    ppermute x4, starting transfers between devices, padded_2(): before = lax.ppermute(last, axis, up)  19.7 us
    all_to_all x1, waiting for transfers between devices, per_device(): lax.all_to_all(products, ('sx', 'sy'), split_axis=0, concat_axis=0, tiled...  19 us
    scatter-add x1, other arithmetic, per_device(): second.reshape(-1, width).at[tile_list].add(alpha * r_tiles)  15.8 us
    reshape x2, local copies, waits for them, and re-layouts, per_device(): second.reshape(-1, width).at[tile_list].add(alpha * r_tiles)  14.1 us
    add x1, other arithmetic, per_device(): second = first + 2.75 * dinv * (rhs - apply_op(first, sigma))  12.7 us
    sub x1, other arithmetic, per_device(): field_res = rhs - apply_op(second, sigma)  12.7 us
  transfers between devices with their start and end apart: 9, of which 4 were waited for; matrix products, arithmetic and copies ran while one was open for 7% of the time, Pallas kernels for 0%

commit v1 on v0

v1 whole, which is shorter than its diff:
```python
import functools

import jax
import jax.numpy as jnp
from jax import lax
from jax.experimental import pallas as pl
from jax.experimental.pallas import tpu as pltpu
from jax.sharding import PartitionSpec as P

MESH = pl.DeviceIdType.MESH
W1 = 0.6111111
W2 = 2.75
CC = W1 + W2 * (1.0 - W1)
LANES = 128
F32 = jnp.float32
BF16 = jnp.bfloat16


def halo_sum(ref, row, col, rows, width):
    if rows == 8:
        ref = ref.at[pl.ds(row, 24)]
        row = 0
    wide = ref[row + 8 : row + 8 + rows, col : col + width + 2 * LANES]
    total = width + 2 * LANES
    left = pltpu.roll(wide, 1, 1)[:, LANES : LANES + width]
    right = pltpu.roll(wide, total - 1, 1)[:, LANES : LANES + width]
    up = ref[row + 7 : row + 7 + rows, col + LANES : col + LANES + width]
    down = ref[row + 9 : row + 9 + rows, col + LANES : col + LANES + width]
    return (left + right) + (up + down)


def spans(c0, c1, step):
    return [(c, min(step, c1 - c)) for c in range(c0, c1, step)]


def front_kernel(nsx, nsy, rhs_h, sig_h, idx_ref, own_ref, sch_ref,
                 sp, cr, r_out, q_out, sums_out,
                 rhs_v, d_v, fp, rb, blocks, row_s, row_r, col_s, col_r, sum_buf,
                 in_sem, hs_sem, hr_sem, ag_r, ss_z, ss_y, ss_x, ss_c, sum_s, sum_r):
    rows, cols = rhs_v.shape
    tiles = r_out.shape[0]
    runs = cols // LANES
    nz, nx = nsx // 2, nsy // 2
    n = nsx * nsy
    sx = lax.axis_index("sx")
    sy = lax.axis_index("sy")
    me = sx * nsy + sy
    z, y = lax.div(sx, 2), lax.rem(sx, 2)
    x, c = lax.div(sy, 2), lax.rem(sy, 2)

    left, right = (0, 2 * LANES), (cols - 2 * LANES, cols)
    regions = [(0, rows) + left, (0, rows) + right,
               (0, 16, left[1], right[0]), (rows - 16, rows, left[1], right[0])]
    chunks = 4
    step = (rows - 32) // chunks // 8 * 8
    cuts = [16 + step * i for i in range(chunks)] + [rows - 16]
    for i in range(chunks):
        regions.append((cuts[i], cuts[i + 1], left[1], right[0]))
    loads = []
    for i, (r0, r1, c0, c1) in enumerate(regions):
        pair = []
        for k, (src, dst) in enumerate(((rhs_h, rhs_v), (sig_h, d_v))):
            cp = pltpu.make_async_copy(src.at[r0:r1, c0:c1], dst.at[r0:r1, c0:c1], in_sem.at[k, i])
            cp.start()
            pair.append(cp)
        loads.append(pair)

    barrier = pltpu.get_barrier_semaphore()

    @pl.loop(1, n)
    def _(k):
        o = lax.rem(me + k, n)
        pl.semaphore_signal(barrier, inc=1, device_id=(lax.div(o, nsy), lax.rem(o, nsy)),
                            device_id_type=MESH)

    blocks[c, (2 * z + y) * nx + x] = sch_ref[...]
    pl.semaphore_wait(barrier, n - 1)

    half = LANES // 2

    def piece(h, zz, yy, xx, cc, dev, sem):
        pair = (2 * zz + yy) * nx + xx
        ref = blocks.at[cc, pair, pl.ds(h * half, half), :]
        dz, dy, dx, dc = dev
        return pltpu.make_async_remote_copy(
            ref, ref, sem, ag_r.at[h, 2 * pair + cc],
            device_id=(2 * dz + dy, 2 * dx + dc), device_id_type=MESH)

    sends = []

    def send(*args):
        cp = piece(*args)
        cp.start()
        sends.append(cp)

    def arrived(h, zz, yy, xx, cc):
        piece(h, zz, yy, xx, cc, (z, y, x, 1 - c), ss_c.at[0, 0, 0, 0]).wait_recv()

    zs = [lax.rem(z + k, nz) for k in range(nz)]
    ys = [y, 1 - y]
    xs = [lax.rem(x + k, nx) for k in range(nx)]

    def to_core(h, i, j, k):
        send(h, zs[i], ys[j], xs[k], c, (z, y, x, 1 - c), ss_c.at[h, i, j, k])

    for h in range(2):
        for i in range(1, nz):
            send(h, z, y, x, c, (zs[i], y, x, c), ss_z.at[h, i])

    def ag_first(i):
        for h in range(2):
            if i:
                arrived(h, zs[i], y, x, c)
            if h == 0:
                send(0, zs[i], y, x, c, (z, 1 - y, x, c), ss_y.at[0, i, 0])
            for k in range(1, nx):
                send(h, zs[i], y, x, c, (z, y, xs[k], c), ss_x.at[h, i, 0, k])
            if h == 1:
                send(1, zs[i], y, x, c, (z, 1 - y, x, c), ss_y.at[1, i, 0])
            to_core(h, i, 0, 0)

    def ag_second(i):
        arrived(0, zs[i], 1 - y, x, c)
        for k in range(1, nx):
            send(0, zs[i], 1 - y, x, c, (z, y, xs[k], c), ss_x.at[0, i, 1, k])
        to_core(0, i, 1, 0)
        for k in range(1, nx):
            arrived(1, zs[i], y, xs[k], c)
            send(1, zs[i], y, xs[k], c, (z, 1 - y, x, c), ss_y.at[1, i, k])
            to_core(1, i, 0, k)

    def ag_third(i):
        for k in range(1, nx):
            arrived(0, zs[i], y, xs[k], c)
            to_core(0, i, 0, k)
            arrived(0, zs[i], 1 - y, xs[k], c)
            to_core(0, i, 1, k)
        for k in range(nx):
            arrived(1, zs[i], 1 - y, xs[k], c)
            to_core(1, i, 1, k)

    def ag_last():
        for h in range(2):
            for i in range(nz):
                for j in range(2):
                    for k in range(nx):
                        arrived(h, zs[i], ys[j], xs[k], 1 - c)

    def do_first(r0, r1, c0, c1):
        @pl.loop(r0 // 8, r1 // 8)
        def _(t):
            r = pl.multiple_of(t * 8, 8)
            for col, w in spans(c0, c1, 512):
                rhs = rhs_v[pl.ds(r, 8), col : col + w]
                dinv = 1.0 / (4.0 + d_v[pl.ds(r, 8), col : col + w])
                d_v[pl.ds(r, 8), col : col + w] = dinv
                fp[pl.ds(r + 8, 8), col + LANES : col + LANES + w] = W1 * dinv * rhs

    def do_second(r0, r1, c0, c1):
        @pl.loop(r0 // 8, r1 // 8)
        def _(t):
            r = pl.multiple_of(t * 8, 8)
            for col, w in spans(c0, c1, 1024):
                beside = halo_sum(fp, r, col, 8, w)
                rhs = rhs_v[pl.ds(r, 8), col : col + w]
                dinv = d_v[pl.ds(r, 8), col : col + w]
                sp[pl.ds(r + 8, 8), col + LANES : col + LANES + w] = dinv * (CC * rhs + W2 * beside)

    lane = lax.broadcasted_iota(jnp.int32, (8, LANES), 1)
    up_dev = (lax.rem(sx + nsx - 1, nsx), sy)
    down_dev = (lax.rem(sx + 1, nsx), sy)
    left_dev = (sx, lax.rem(sy + nsy - 1, nsy))
    right_dev = (sx, lax.rem(sy + 1, nsy))

    def halo_copies(ph):
        out = []
        for k, dev in enumerate((up_dev, down_dev)):
            out.append(pltpu.make_async_remote_copy(
                row_s.at[ph, k], row_r.at[ph, k], hs_sem.at[ph, k], hr_sem.at[ph, k],
                device_id=dev, device_id_type=MESH))
        for k, dev in enumerate((left_dev, right_dev)):
            out.append(pltpu.make_async_remote_copy(
                col_s.at[ph, k], col_r.at[ph, k], hs_sem.at[ph, 2 + k], hr_sem.at[ph, 2 + k],
                device_id=dev, device_id_type=MESH))
        return out

    def halo_send(ph, ref):
        row_s[ph, 0] = ref[8:9, LANES : LANES + cols]
        row_s[ph, 1] = ref[rows + 7 : rows + 8, LANES : LANES + cols]
        one = jnp.zeros((8, LANES), F32)
        two = jnp.zeros((8, LANES), F32)
        for i in range(rows // 8):
            a = ref[8 + 8 * i : 16 + 8 * i, LANES : 2 * LANES]
            b = ref[8 + 8 * i : 16 + 8 * i, cols : cols + LANES]
            one = jnp.where(lane == i, a[:, 0:1], one)
            two = jnp.where(lane == i, b[:, LANES - 1 : LANES], two)
        col_s[ph, 0] = one
        col_s[ph, 1] = two
        cps = halo_copies(ph)
        for cp in cps:
            cp.start()
        return cps

    def halo_take(ph, ref, cps):
        for cp in cps:
            cp.wait_recv()
        zero_row = jnp.zeros((1, cols), F32)
        ref[7:8, LANES : LANES + cols] = jnp.where(sx > 0, row_r[ph, 1], zero_row)
        ref[rows + 8 : rows + 9, LANES : LANES + cols] = jnp.where(sx < nsx - 1, row_r[ph, 0], zero_row)
        zero = jnp.zeros((8, LANES), F32)
        from_left = jnp.where(sy > 0, col_r[ph, 1], zero)
        from_right = jnp.where(sy < nsy - 1, col_r[ph, 0], zero)
        for i in range(rows // 8):
            ref[8 + 8 * i : 16 + 8 * i, 0:LANES] = jnp.broadcast_to(from_left[:, i : i + 1], (8, LANES))
            ref[8 + 8 * i : 16 + 8 * i, cols + LANES : cols + 2 * LANES] = jnp.broadcast_to(
                from_right[:, i : i + 1], (8, LANES))

    for i in range(4):
        for cp in loads[i]:
            cp.wait()
        do_first(*regions[i])
    cps0 = halo_send(0, fp)
    ag_first(0)
    for cp in loads[4]:
        cp.wait()
    do_first(*regions[4])
    for i in range(1, nz):
        ag_first(i)
    halo_take(0, fp, cps0)
    do_second(0, rows, *left)
    do_second(0, rows, *right)
    do_second(0, 8, LANES, cols - LANES)
    do_second(rows - 8, rows, LANES, cols - LANES)
    cps1 = halo_send(1, sp)
    for i in range(nz):
        ag_second(i)
    for i in range(5, 4 + chunks):
        for cp in loads[i]:
            cp.wait()
        do_first(*regions[i])
    for i in range(nz):
        ag_third(i)

    index = idx_ref[...]
    owner = own_ref[...]
    trow = lax.div(index, runs)
    tcol = index - trow * runs
    rid = jnp.where(tcol == 0, trow, jnp.where(tcol == runs - 1, rows + trow, jnp.where(
        trow == 0, 2 * rows + tcol, 2 * rows + runs + tcol)))
    ra = lax.shift_right_logical(rid, 7)
    rbm = rid & (LANES - 1)
    pr = lax.shift_right_logical(owner, 1)
    par = owner & 1
    nblk = tiles // LANES
    stack = jnp.concatenate([v.astype(F32) for v in (ra, rbm, pr, par)]
                            + [jnp.zeros((LANES - 4 * nblk, LANES), F32)], axis=0)
    numbers = stack.T

    halo_take(1, sp, cps1)

    def rim(row, col, nrows, width):
        return ((1.0 - CC) * rhs_v[pl.ds(row, nrows), col : col + width]
                - W2 * halo_sum(fp, row, col, nrows, width) + halo_sum(sp, row, col, nrows, width))

    def put(at, nrows, value):
        cr[pl.ds(at, nrows), :] = value

    @pl.loop(0, rows // 16)
    def _(t):
        for u in range(2):
            r = pl.multiple_of(t * 16 + u * 8, 8)
            put(r, 8, rim(r, 0, 8, LANES))
            put(r + rows, 8, rim(r, cols - LANES, 8, LANES))

    cr[2 * rows :, :] = jnp.zeros((cr.shape[0] - 2 * rows, LANES), F32)
    top = rim(0, 0, 1, cols)
    bottom = rim(rows - 1, 0, 1, cols)
    for k in range(runs):
        put(2 * rows + k, 1, top[:, LANES * k : LANES * k + LANES])
        put(2 * rows + runs + k, 1, bottom[:, LANES * k : LANES * k + LANES])

    nk = cr.shape[0] // LANES

    @pl.loop(0, nk)
    def _(t):
        at = pl.multiple_of(t * LANES, LANES)
        v = cr[pl.ds(at, LANES), :]
        hi = v.astype(BF16)
        rb[pl.ds(at, LANES), 0:LANES] = hi
        rb[pl.ds(at, LANES), LANES:] = (v - hi.astype(F32)).astype(BF16)

    ag_last()
    m = 4
    lanes_m = lax.broadcasted_iota(jnp.int32, (m * LANES, LANES), 1).astype(F32)
    zero_b = jnp.zeros((m * LANES, LANES), BF16)
    count = jnp.zeros((LANES, LANES), F32)
    rr = jnp.zeros((8, LANES), F32)
    pq = jnp.zeros((8, LANES), F32)
    qq = jnp.zeros((8, LANES), F32)

    def spread(kind, g):
        return jnp.concatenate([
            jnp.broadcast_to(numbers[:, kind * nblk + g * m + u : kind * nblk + g * m + u + 1],
                             (LANES, LANES)) for u in range(m)], axis=0)

    def fold(v):
        return jnp.sum(v.reshape(-1, 8, LANES), axis=0)

    npair = blocks.shape[1]
    gp = min(npair, 16)
    for g in range(nblk // m):
        at = g * m * LANES
        a32 = spread(0, g)
        a16 = a32.astype(BF16)
        base = jnp.where(spread(1, g) == lanes_m, 1.0, 0.0).astype(BF16)
        aone = jnp.where(a32 == lanes_m, 1.0, 0.0).astype(BF16)
        count += lax.dot_general(base, aone, (((0,), (0,)), ((), ())), preferred_element_type=F32)
        hot = jnp.concatenate([jnp.where(a16 == k, base, zero_b) for k in range(nk)], axis=1)
        both = jnp.dot(hot, rb[...], preferred_element_type=F32)
        r = both[:, :LANES] + both[:, LANES:]
        p = both[:, :LANES].astype(BF16)
        r_out[at : at + m * LANES, :] = r
        p16 = spread(2, g).astype(BF16)

        def pairs(k0, acc):
            masked = jnp.concatenate(
                [jnp.where(p16 == (k0 + k if isinstance(k0, int) else (k0 + k).astype(BF16)), p, zero_b)
                 for k in range(gp)], axis=1)
            mats = jnp.concatenate([blocks[0, pl.ds(k0, gp)].reshape(gp * LANES, LANES),
                                    blocks[1, pl.ds(k0, gp)].reshape(gp * LANES, LANES)], axis=1)
            return acc + jnp.dot(masked, mats, preferred_element_type=F32)

        acc = jnp.zeros((m * LANES, 2 * LANES), F32)
        if npair == gp:
            acc = pairs(0, acc)
        else:
            acc = lax.fori_loop(0, npair // gp, lambda s, v: pairs(s * gp, v), acc)
        qb = jnp.where(spread(3, g) > 0.5, acc[:, LANES:], acc[:, :LANES]).astype(BF16)
        q_out[at : at + m * LANES, :] = qb
        q = qb.astype(F32)
        rr += fold(r * r)
        pq += fold(r * q)
        qq += fold(q * q)

    part = jnp.concatenate([jnp.sum(v, axis=0, keepdims=True) for v in (rr, pq, qq)]
                           + [jnp.zeros((5, LANES), F32)], axis=0)
    sum_buf[me] = part

    def sum_copy(slot, k):
        o = lax.rem(me + k, n)
        return pltpu.make_async_remote_copy(
            sum_buf.at[slot], sum_buf.at[slot], sum_s.at[k], sum_r.at[slot],
            device_id=(lax.div(o, nsy), lax.rem(o, nsy)), device_id_type=MESH)

    @pl.loop(1, n)
    def _(k):
        sum_copy(me, k).start()

    do_second(8, rows - 8, LANES, cols - LANES)
    for a in range(nk):
        at = a * LANES
        cr[at : at + LANES, :] = cr[at : at + LANES, :] * count[:, a : a + 1]

    for cp in cps0 + cps1:
        cp.wait_send()
    for cp in sends:
        cp.wait_send()

    @pl.loop(1, n)
    def _(k):
        sum_copy(me, k).wait_send()
        sum_copy(lax.rem(me + k, n), k).wait_recv()

    sums_out[...] = jnp.sum(sum_buf[...], axis=0)


def back_kernel(sp, cr, r_ref, q_ref, sums, out, res, direc,
                left, right, top, bottom, res_v, dir_v, sem):
    rows, cols = out.shape
    tiles = r_ref.shape[0]
    runs = cols // LANES
    inner = pltpu.make_async_copy(
        sp.at[16 : rows, 2 * LANES : cols],
        out.at[8 : rows - 8, LANES : cols - LANES], sem.at[0])
    inner.start()
    copies = [inner]
    total = jnp.sum(sums[...], axis=1, keepdims=True)
    rr, pq, qq = total[0:1], total[1:2], total[2:3]
    alpha = rr / pq
    beta = (rr - 2.0 * alpha * pq + alpha * alpha * qq) / rr

    nch = 4
    size = tiles // nch
    for k in range(nch):
        sl = slice(k * size, (k + 1) * size)

        @pl.loop(0, size // 64)
        def _(t, k=k):
            at = pl.multiple_of(k * size + t * 64, 64)
            r = r_ref[pl.ds(at, 64), :]
            v = r - alpha * q_ref[pl.ds(at, 64), :].astype(F32)
            res_v[pl.ds(at, 64), :] = v
            dir_v[pl.ds(at, 64), :] = v + beta * r

        for src, dst, i in ((res_v, res, 1 + k), (dir_v, direc, 1 + nch + k)):
            cp = pltpu.make_async_copy(src.at[sl], dst.at[sl], sem.at[i])
            cp.start()
            copies.append(cp)

    @pl.loop(0, rows // 64)
    def _(t):
        at = pl.multiple_of(t * 64, 64)
        left[pl.ds(at, 64), :] = sp[pl.ds(at + 8, 64), LANES : 2 * LANES] + alpha * cr[pl.ds(at, 64), :]
        right[pl.ds(at, 64), :] = (sp[pl.ds(at + 8, 64), cols : cols + LANES]
                                   + alpha * cr[pl.ds(at + rows, 64), :])

    top[...] = sp[8:16, 2 * LANES : cols]
    bottom[...] = sp[rows : rows + 8, 2 * LANES : cols]
    for k in range(1, runs - 1):
        sl = slice((k - 1) * LANES, k * LANES)
        top[0:1, sl] = top[0:1, sl] + alpha * cr[2 * rows + k : 2 * rows + k + 1, :]
        bottom[7:8, sl] = bottom[7:8, sl] + alpha * cr[2 * rows + runs + k : 2 * rows + runs + k + 1, :]
    i = 1 + 2 * nch
    for src, dst in ((left, out.at[:, 0:LANES]), (right, out.at[:, cols - LANES : cols]),
                     (top, out.at[0:8, LANES : cols - LANES]),
                     (bottom, out.at[rows - 8 : rows, LANES : cols - LANES])):
        cp = pltpu.make_async_copy(src, dst, sem.at[i])
        cp.start()
        copies.append(cp)
        i += 1
    for cp in copies:
        cp.wait()


def per_device(nsx, nsy, rhs, sigma, tile_list, tile_owner, schur_blocks):
    rows, cols = rhs.shape
    tiles = tile_list.shape[0]
    n = nsx * nsy
    nz, nx = nsx // 2, nsy // 2
    nk = -(-(2 * rows + 2 * (cols // LANES)) // LANES)
    vm = pl.BlockSpec(memory_space=pltpu.VMEM)
    hbm = pl.BlockSpec(memory_space=pl.ANY)
    dma = pltpu.SemaphoreType.DMA
    padded = (rows + 16, cols + 2 * LANES)
    kept = pltpu.VMEM
    sp, cr, r, q, sums = pl.pallas_call(
        functools.partial(front_kernel, nsx, nsy),
        out_shape=[kept(padded, F32), kept((nk * LANES, LANES), F32), kept((tiles, LANES), F32),
                   kept((tiles, LANES), BF16), kept((8, LANES), F32)],
        in_specs=[hbm, hbm, vm, vm, vm],
        out_specs=[vm] * 5,
        scratch_shapes=[
            pltpu.VMEM((rows, cols), F32), pltpu.VMEM((rows, cols), F32), pltpu.VMEM(padded, F32),
            pltpu.VMEM((nk * LANES, 2 * LANES), BF16), pltpu.VMEM((2, n // 2, LANES, LANES), BF16),
            pltpu.VMEM((2, 2, 1, cols), F32), pltpu.VMEM((2, 2, 1, cols), F32),
            pltpu.VMEM((2, 2, 8, LANES), F32), pltpu.VMEM((2, 2, 8, LANES), F32),
            pltpu.VMEM((n, 8, LANES), F32),
            dma((2, 8)), dma((2, 4)), dma((2, 4)), dma((2, n)), dma((2, nz)), dma((2, nz, nx)),
            dma((2, nz, 2, nx)), dma((2, nz, 2, nx)), dma((n,)), dma((n,)),
        ],
        compiler_params=pltpu.CompilerParams(
            collective_id=0, has_side_effects=True, vmem_limit_bytes=44 * 2**20),
        name="front",
    )(rhs, sigma, tile_list.reshape(-1, LANES), tile_owner.reshape(-1, LANES),
      schur_blocks.reshape(LANES, LANES))
    nch = 4
    return pl.pallas_call(
        back_kernel,
        out_shape=[jax.ShapeDtypeStruct((rows, cols), F32), jax.ShapeDtypeStruct((tiles, LANES), F32),
                   jax.ShapeDtypeStruct((tiles, LANES), F32)],
        in_specs=[vm] * 5,
        out_specs=[hbm] * 3,
        scratch_shapes=[
            pltpu.VMEM((rows, LANES), F32), pltpu.VMEM((rows, LANES), F32),
            pltpu.VMEM((8, cols - 2 * LANES), F32), pltpu.VMEM((8, cols - 2 * LANES), F32),
            pltpu.VMEM((tiles, LANES), F32), pltpu.VMEM((tiles, LANES), F32),
            dma((1 + 2 * nch + 4,)),
        ],
        compiler_params=pltpu.CompilerParams(vmem_limit_bytes=16 * 2**20),
        name="back",
    )(sp, cr, r, q, sums)


def solution(mesh):
    nsx, nsy = mesh.shape["sx"], mesh.shape["sy"]
    in_specs = (
        P("sx", "sy"),
        P("sx", "sy"),
        P(("sx", "sy")),
        P(("sx", "sy"), None),
        P(("sx", "sy"), None, None),
    )
    out_specs = (P("sx", "sy"), P(("sx", "sy"), None), P(("sx", "sy"), None))

    def body(*args):
        return tuple(per_device(nsx, nsy, *args))

    return jax.shard_map(body, mesh=mesh, in_specs=in_specs, out_specs=out_specs, check_vma=False)
```

time: 245 us -> 65.2 us (0.27)
  blocking collectives: 80.4 us -> 0 us
  other arithmetic: 66.8 us -> 0 us
  Pallas kernels: 0 us -> 62.1 us
  local copies, waits for them, and re-layouts: 38.8 us -> 2.14 us
  starting transfers between devices: 28.8 us -> 0 us
  waiting for transfers between devices: 22.7 us -> 0 us
  between operations: 4.9 us -> 0.65 us
    pallas_call x0 -> x2, Pallas kernels: none -> 62.1 us  [the longest x1 58.7 us: per_device(): pl.pallas_call(functools.partial(front_kernel, nsx, nsy), out_shape=[kept...]
    all_to_all x1 -> x0, blocking collectives: 41.6 us -> none  [per_device(): lax.all_to_all(boxed, ('sx', 'sy'), split_axis=0, concat_axis=0, tiled=True)]
    psum x1 -> x0, blocking collectives: 38.8 us -> none  [per_device(): lax.psum((jnp.sum(r_tiles * r_tiles), jnp.sum(r_tiles * q_tiles), jnp.sum...]
    ppermute x8 -> x0, starting transfers between devices: 25 us -> none  [the longest x4 19.7 us: padded_2(): before = lax.ppermute(last, axis, up)]
    reshape x3 -> x0, local copies, waits for them, and re-layouts: 21.2 us -> none  [the longest x2 14.1 us: per_device(): second.reshape(-1, width).at[tile_list].add(alpha * r_tiles)]
    all_to_all x1 -> x0, waiting for transfers between devices: 19 us -> none  [per_device(): lax.all_to_all(products, ('sx', 'sy'), split_axis=0, concat_axis=0, tiled...]
    scatter-add x1 -> x0, other arithmetic: 15.8 us -> none  [per_device(): second.reshape(-1, width).at[tile_list].add(alpha * r_tiles)]
    gather x2 -> x0, local copies, waits for them, and re-layouts: 14.4 us -> none  [the longest x1 8.24 us: per_device(): r_tiles = field_res.reshape(-1, width)[tile_list]]
  transfers between devices with their start and end apart: 9 -> 0, of which waited for: 4 -> 0; matrix products, arithmetic and copies ran while one was open for 7% -> 0% of each run, Pallas kernels for 0% -> 0%
where the time goes in v1:
time: 65.2 us; the launch traced here: 64.9 us
  Pallas kernels  62.1 us (95%)
  local copies, waits for them, and re-layouts  2.14 us (3%)
    pallas_call x1, Pallas kernels, per_device(): pl.pallas_call(functools.partial(front_kernel, nsx, nsy), out_shape=[kept...  58.7 us
    pallas_call x1, Pallas kernels, per_device(): pl.pallas_call(back_kernel, out_shape=[jax.ShapeDtypeStruct((rows, cols),...  3.4 us
    unnamed x6, local copies, waits for them, and re-layouts  2.14 us

profile of v1, /device:TPU:0, one launch (start us, length us, event | category | flops | bytes accessed | tf_op | source)
XLA Modules:
  0.0 64.9 jit_solution(10712257511422511989)
XLA Ops:
  0.6 0.0 copy-start
  0.6 0.7 %copy-done = bf16[1,128,128]{2,1,0:T(8,128)(2,1)S(1)} copy-done((bf16[1,128,128]{2,1,0:T(8,128)(2,1)S(1)}, bf16[1,128,128]{2,1,0:T(8,128)(2,1)}, u32[]{:S(2)}) %copy-start) | copy-done | bytes 32792
  1.4 0.0 copy-start.1
  1.4 0.7 %copy-done.1 = s32[2048]{0:T(1024)S(1)} copy-done((s32[2048]{0:T(1024)S(1)}, s32[2048]{0:T(1024)}, u32[]{:S(2)}) %copy-start.1) | copy-done | bytes 8216
  2.1 0.0 copy-start.2
  2.1 0.7 %copy-done.2 = s32[2048,1]{0,1:T(1,128)S(1)} copy-done((s32[2048,1]{0,1:T(1,128)S(1)}, s32[2048,1]{0,1:T(1,128)}, u32[]{:S(2)}) %copy-start.2) | copy-done | bytes 8216
  2.8 58.7 %front.1 = (f32[784,2304]{1,0:T(8,128)S(1)}, f32[1664,128]{1,0:T(8,128)S(1)}, f32[2048,128]{1,0:T(8,128)S(1)}, bf16[2048,128]{1,0:T(8,128)(2,1)S(1)}, f32[8,128]{1,0:T(8,128)S(1)}) custom-call(f32[768,2048]{1,0:T(8,128)} %rhs_h.1, f32[768,2048]{1,0:T(8,128)} %sig_h.1, s32[16,128]{1,0:T(8,128)S(1)} %bitcast.4, s32[16,128]{1,0:T(8,128)S(1)} %bitcast.5, ...), custom_call_target="tpu_custom_call" | custom-call | tf_op jit(solution)/shard_map/front/pallas_call | solution.py:446
  61.5 3.4 %back.1 = (f32[768,2048]{1,0:T(8,128)}, f32[2048,128]{1,0:T(8,128)}, f32[2048,128]{1,0:T(8,128)}) custom-call(f32[784,2304]{1,0:T(8,128)S(1)} %get-tuple-element.8.sp, f32[1664,128]{1,0:T(8,128)S(1)} %get-tuple-element.9.cr, f32[2048,128]{1,0:T(8,128)S(1)} %get-tuple-element.10.r_ref, bf16[2048,128]{1,0:T(8,128)(2,1)S(1)} %get-tuple-element.11.q_ref, ...), custom_call_target="tpu_custom_call" | custom-call | tf_op jit(solution)/shard_map/back/pallas_call | solution.py:467
Async XLA Ops:
  0.6 0.8 %copy-start = (bf16[1,128,128]{2,1,0:T(8,128)(2,1)S(1)}, bf16[1,128,128]{2,1,0:T(8,128)(2,1)}, u32[]{:S(2)}) copy-start(bf16[1,128,128]{2,1,0:T(8,128)(2,1)} %param.9) | copy-start | bytes 98308
  1.4 0.7 %copy-start.1 = (s32[2048]{0:T(1024)S(1)}, s32[2048]{0:T(1024)}, u32[]{:S(2)}) copy-start(s32[2048]{0:T(1024)} %param.7) | copy-start | bytes 24580
  2.1 0.7 %copy-start.2 = (s32[2048,1]{0,1:T(1,128)S(1)}, s32[2048,1]{0,1:T(1,128)}, u32[]{:S(2)}) copy-start(s32[2048,1]{0,1:T(1,128)} %param.8) | copy-start | bytes 24580

commit v2 on v1

--- a/solution.py
+++ b/solution.py
@@ -17,8 +17,8 @@
 
 
 def halo_sum(ref, row, col, rows, width):
-    if rows == 8:
-        ref = ref.at[pl.ds(row, 24)]
+    if not isinstance(row, int):
+        ref = ref.at[pl.ds(row, rows + 16)]
         row = 0
     wide = ref[row + 8 : row + 8 + rows, col : col + width + 2 * LANES]
     total = width + 2 * LANES
@@ -29,14 +29,10 @@
     return (left + right) + (up + down)
 
 
-def spans(c0, c1, step):
-    return [(c, min(step, c1 - c)) for c in range(c0, c1, step)]
-
-
 def front_kernel(nsx, nsy, rhs_h, sig_h, idx_ref, own_ref, sch_ref,
                  sp, cr, r_out, q_out, sums_out,
-                 rhs_v, d_v, fp, rb, blocks, row_s, row_r, col_s, col_r, sum_buf,
-                 in_sem, hs_sem, hr_sem, ag_r, ss_z, ss_y, ss_x, ss_c, sum_s, sum_r):
+                 rhs_v, d_v, fp, rb, blocks, idx_v, own_v, p_v, row_s, row_r, col_s, col_r, sum_buf,
+                 in_sem, small_sem, hs_sem, hr_sem, ag_r, ss_z, ss_y, ss_x, ss_c, sum_s, sum_r):
     rows, cols = rhs_v.shape
     tiles = r_out.shape[0]
     runs = cols // LANES
@@ -52,7 +48,7 @@
     regions = [(0, rows) + left, (0, rows) + right,
                (0, 16, left[1], right[0]), (rows - 16, rows, left[1], right[0])]
     chunks = 4
-    step = (rows - 32) // chunks // 8 * 8
+    step = (rows - 32) // chunks // 16 * 16
     cuts = [16 + step * i for i in range(chunks)] + [rows - 16]
     for i in range(chunks):
         regions.append((cuts[i], cuts[i + 1], left[1], right[0]))
@@ -73,8 +69,10 @@
         pl.semaphore_signal(barrier, inc=1, device_id=(lax.div(o, nsy), lax.rem(o, nsy)),
                             device_id_type=MESH)
 
-    blocks[c, (2 * z + y) * nx + x] = sch_ref[...]
-    pl.semaphore_wait(barrier, n - 1)
+    small = [pltpu.make_async_copy(src, dst, small_sem.at[i]) for i, (src, dst) in enumerate((
+        (sch_ref, blocks.at[c, (2 * z + y) * nx + x]), (idx_ref, idx_v), (own_ref, own_v)))]
+    for cp in small:
+        cp.start()
 
     half = LANES // 2
 
@@ -102,10 +100,6 @@
 
     def to_core(h, i, j, k):
         send(h, zs[i], ys[j], xs[k], c, (z, y, x, 1 - c), ss_c.at[h, i, j, k])
-
-    for h in range(2):
-        for i in range(1, nz):
-            send(h, z, y, x, c, (zs[i], y, x, c), ss_z.at[h, i])
 
     def ag_first(i):
         for h in range(2):
@@ -146,25 +140,29 @@
                     for k in range(nx):
                         arrived(h, zs[i], ys[j], xs[k], 1 - c)
 
-    def do_first(r0, r1, c0, c1):
-        @pl.loop(r0 // 8, r1 // 8)
+    def do_first(r0, r1, c0, c1, b):
+        w = c1 - c0
+
+        @pl.loop(0, (r1 - r0) // b)
         def _(t):
-            r = pl.multiple_of(t * 8, 8)
-            for col, w in spans(c0, c1, 512):
-                rhs = rhs_v[pl.ds(r, 8), col : col + w]
-                dinv = 1.0 / (4.0 + d_v[pl.ds(r, 8), col : col + w])
-                d_v[pl.ds(r, 8), col : col + w] = dinv
-                fp[pl.ds(r + 8, 8), col + LANES : col + LANES + w] = W1 * dinv * rhs
-
-    def do_second(r0, r1, c0, c1):
-        @pl.loop(r0 // 8, r1 // 8)
+            r = pl.multiple_of(r0 + t * b, 8)
+            rhs = rhs_v[pl.ds(r, b), c0:c1]
+            diag = 4.0 + d_v[pl.ds(r, b), c0:c1]
+            near = pl.reciprocal(diag, approx=True)
+            dinv = near * (2.0 - diag * near)
+            d_v[pl.ds(r, b), c0:c1] = dinv
+            fp[pl.ds(r + 8, b), c0 + LANES : c0 + LANES + w] = W1 * dinv * rhs
+
+    def do_second(r0, r1, c0, c1, b):
+        w = c1 - c0
+
+        @pl.loop(0, (r1 - r0) // b)
         def _(t):
-            r = pl.multiple_of(t * 8, 8)
-            for col, w in spans(c0, c1, 1024):
-                beside = halo_sum(fp, r, col, 8, w)
-                rhs = rhs_v[pl.ds(r, 8), col : col + w]
-                dinv = d_v[pl.ds(r, 8), col : col + w]
-                sp[pl.ds(r + 8, 8), col + LANES : col + LANES + w] = dinv * (CC * rhs + W2 * beside)
+            r = pl.multiple_of(r0 + t * b, 8)
+            beside = halo_sum(fp, r, c0, b, w)
+            rhs = rhs_v[pl.ds(r, b), c0:c1]
+            dinv = d_v[pl.ds(r, b), c0:c1]
+            sp[pl.ds(r + 8, b), c0 + LANES : c0 + LANES + w] = dinv * (CC * rhs + W2 * beside)
 
     lane = lax.broadcasted_iota(jnp.int32, (8, LANES), 1)
     up_dev = (lax.rem(sx + nsx - 1, nsx), sy)
@@ -218,31 +216,37 @@
     for i in range(4):
         for cp in loads[i]:
             cp.wait()
-        do_first(*regions[i])
+        do_first(*regions[i], 32 if i < 2 else 16)
+    for cp in small:
+        cp.wait()
+    pl.semaphore_wait(barrier, n - 1)
+    for h in range(2):
+        for i in range(1, nz):
+            send(h, z, y, x, c, (zs[i], y, x, c), ss_z.at[h, i])
     cps0 = halo_send(0, fp)
     ag_first(0)
     for cp in loads[4]:
         cp.wait()
-    do_first(*regions[4])
+    do_first(*regions[4], 16)
     for i in range(1, nz):
         ag_first(i)
     halo_take(0, fp, cps0)
-    do_second(0, rows, *left)
-    do_second(0, rows, *right)
-    do_second(0, 8, LANES, cols - LANES)
-    do_second(rows - 8, rows, LANES, cols - LANES)
+    do_second(0, rows, *left, 32)
+    do_second(0, rows, *right, 32)
+    do_second(0, 8, LANES, cols - LANES, 8)
+    do_second(rows - 8, rows, LANES, cols - LANES, 8)
     cps1 = halo_send(1, sp)
     for i in range(nz):
         ag_second(i)
     for i in range(5, 4 + chunks):
         for cp in loads[i]:
             cp.wait()
-        do_first(*regions[i])
+        do_first(*regions[i], 16)
     for i in range(nz):
         ag_third(i)
 
-    index = idx_ref[...]
-    owner = own_ref[...]
+    index = idx_v[...]
+    owner = own_v[...]
     trow = lax.div(index, runs)
     tcol = index - trow * runs
     rid = jnp.where(tcol == 0, trow, jnp.where(tcol == runs - 1, rows + trow, jnp.where(
@@ -265,12 +269,13 @@
     def put(at, nrows, value):
         cr[pl.ds(at, nrows), :] = value
 
-    @pl.loop(0, rows // 16)
+    @pl.loop(0, rows // 32)
     def _(t):
-        for u in range(2):
-            r = pl.multiple_of(t * 16 + u * 8, 8)
-            put(r, 8, rim(r, 0, 8, LANES))
-            put(r + rows, 8, rim(r, cols - LANES, 8, LANES))
+        r = pl.multiple_of(t * 32, 32)
+        one = rim(r, 0, 32, LANES)
+        two = rim(r, cols - LANES, 32, LANES)
+        put(r, 32, one)
+        put(r + rows, 32, two)
 
     cr[2 * rows :, :] = jnp.zeros((cr.shape[0] - 2 * rows, LANES), F32)
     top = rim(0, 0, 1, cols)
@@ -289,7 +294,6 @@
         rb[pl.ds(at, LANES), 0:LANES] = hi
         rb[pl.ds(at, LANES), LANES:] = (v - hi.astype(F32)).astype(BF16)
 
-    ag_last()
     m = 4
     lanes_m = lax.broadcasted_iota(jnp.int32, (m * LANES, LANES), 1).astype(F32)
     zero_b = jnp.zeros((m * LANES, LANES), BF16)
@@ -318,8 +322,15 @@
         hot = jnp.concatenate([jnp.where(a16 == k, base, zero_b) for k in range(nk)], axis=1)
         both = jnp.dot(hot, rb[...], preferred_element_type=F32)
         r = both[:, :LANES] + both[:, LANES:]
-        p = both[:, :LANES].astype(BF16)
+        p_v[at : at + m * LANES, :] = both[:, :LANES].astype(BF16)
         r_out[at : at + m * LANES, :] = r
+        rr += fold(r * r)
+
+    ag_last()
+    for g in range(nblk // m):
+        at = g * m * LANES
+        p = p_v[at : at + m * LANES, :]
+        r = r_out[at : at + m * LANES, :]
         p16 = spread(2, g).astype(BF16)
 
         def pairs(k0, acc):
@@ -338,7 +349,6 @@
         qb = jnp.where(spread(3, g) > 0.5, acc[:, LANES:], acc[:, :LANES]).astype(BF16)
         q_out[at : at + m * LANES, :] = qb
         q = qb.astype(F32)
-        rr += fold(r * r)
         pq += fold(r * q)
         qq += fold(q * q)
 
@@ -356,7 +366,7 @@
     def _(k):
         sum_copy(me, k).start()
 
-    do_second(8, rows - 8, LANES, cols - LANES)
+    do_second(8, rows - 8, LANES, cols - LANES, 16)
     for a in range(nk):
         at = a * LANES
         cr[at : at + LANES, :] = cr[at : at + LANES, :] * count[:, a : a + 1]
@@ -440,6 +450,7 @@
     nk = -(-(2 * rows + 2 * (cols // LANES)) // LANES)
     vm = pl.BlockSpec(memory_space=pltpu.VMEM)
     hbm = pl.BlockSpec(memory_space=pl.ANY)
+    big = pl.BlockSpec(memory_space=pltpu.HBM)
     dma = pltpu.SemaphoreType.DMA
     padded = (rows + 16, cols + 2 * LANES)
     kept = pltpu.VMEM
@@ -447,22 +458,25 @@
         functools.partial(front_kernel, nsx, nsy),
         out_shape=[kept(padded, F32), kept((nk * LANES, LANES), F32), kept((tiles, LANES), F32),
                    kept((tiles, LANES), BF16), kept((8, LANES), F32)],
-        in_specs=[hbm, hbm, vm, vm, vm],
+        in_specs=[big] * 5,
         out_specs=[vm] * 5,
         scratch_shapes=[
             pltpu.VMEM((rows, cols), F32), pltpu.VMEM((rows, cols), F32), pltpu.VMEM(padded, F32),
             pltpu.VMEM((nk * LANES, 2 * LANES), BF16), pltpu.VMEM((2, n // 2, LANES, LANES), BF16),
+            pltpu.VMEM((tiles // LANES, LANES), jnp.int32), pltpu.VMEM((tiles // LANES, LANES), jnp.int32),
+            pltpu.VMEM((tiles, LANES), BF16),
             pltpu.VMEM((2, 2, 1, cols), F32), pltpu.VMEM((2, 2, 1, cols), F32),
             pltpu.VMEM((2, 2, 8, LANES), F32), pltpu.VMEM((2, 2, 8, LANES), F32),
             pltpu.VMEM((n, 8, LANES), F32),
-            dma((2, 8)), dma((2, 4)), dma((2, 4)), dma((2, n)), dma((2, nz)), dma((2, nz, nx)),
+            dma((2, 8)), dma((3,)), dma((2, 4)), dma((2, 4)), dma((2, n)), dma((2, nz)), dma((2, nz, nx)),
             dma((2, nz, 2, nx)), dma((2, nz, 2, nx)), dma((n,)), dma((n,)),
         ],
         compiler_params=pltpu.CompilerParams(
             collective_id=0, has_side_effects=True, vmem_limit_bytes=44 * 2**20),
         name="front",
-    )(rhs, sigma, tile_list.reshape(-1, LANES), tile_owner.reshape(-1, LANES),
-      schur_blocks.reshape(LANES, LANES))
+    )(*[pltpu.with_memory_space_constraint(v, pltpu.HBM) for v in (
+        rhs, sigma, tile_list.reshape(-1, LANES), tile_owner.reshape(-1, LANES),
+        schur_blocks.reshape(LANES, LANES))])
     nch = 4
     return pl.pallas_call(
         back_kernel,

time: 65.2 us -> 46.7 us (0.72)
  Pallas kernels: 62.1 us -> 45.9 us
  local copies, waits for them, and re-layouts: 2.14 us -> 0 us
    pallas_call x1, Pallas kernels: 58.7 us -> 42.5 us  [per_device(): pl.pallas_call(functools.partial(front_kernel, nsx, nsy), out_shape=[kept...]
    unnamed x6 -> x0, local copies, waits for them, and re-layouts: 2.14 us -> none
where the time goes in v2:
time: 46.7 us; the launch traced here: 46.6 us
  Pallas kernels  45.9 us (98%)
  between operations  0.64 us (1%)
    pallas_call x1, Pallas kernels, per_device(): pl.pallas_call(functools.partial(front_kernel, nsx, nsy), out_shape=[kept...  42.5 us
    pallas_call x1, Pallas kernels, per_device(): pl.pallas_call(back_kernel, out_shape=[jax.ShapeDtypeStruct((rows, cols),...  3.4 us

profile of v2, /device:TPU:0, one launch (start us, length us, event | category | flops | bytes accessed | tf_op | source)
XLA Modules:
  0.0 46.6 jit_solution(17276659265439678865)
XLA Ops:
  0.6 42.5 %front.1 = (f32[784,2304]{1,0:T(8,128)S(1)}, f32[1664,128]{1,0:T(8,128)S(1)}, f32[2048,128]{1,0:T(8,128)S(1)}, bf16[2048,128]{1,0:T(8,128)(2,1)S(1)}, f32[8,128]{1,0:T(8,128)S(1)}) custom-call(f32[768,2048]{1,0:T(8,128)} %rhs_h.1, f32[768,2048]{1,0:T(8,128)} %sig_h.1, s32[16,128]{1,0:T(8,128)} %bitcast.4, s32[16,128]{1,0:T(8,128)} %bitcast.5, ...), custom_call_target="tpu_custom_call" | custom-call | tf_op jit(solution)/shard_map/front/pallas_call | solution.py:457
  43.2 3.4 %back.1 = (f32[768,2048]{1,0:T(8,128)}, f32[2048,128]{1,0:T(8,128)}, f32[2048,128]{1,0:T(8,128)}) custom-call(f32[784,2304]{1,0:T(8,128)S(1)} %get-tuple-element.8.sp, f32[1664,128]{1,0:T(8,128)S(1)} %get-tuple-element.9.cr, f32[2048,128]{1,0:T(8,128)S(1)} %get-tuple-element.10.r_ref, bf16[2048,128]{1,0:T(8,128)(2,1)S(1)} %get-tuple-element.11.q_ref, ...), custom_call_target="tpu_custom_call" | custom-call | tf_op jit(solution)/shard_map/back/pallas_call | solution.py:481

commit v3 on v2

--- a/solution.py
+++ b/solution.py
@@ -29,12 +29,10 @@
     return (left + right) + (up + down)
 
 
-def front_kernel(nsx, nsy, rhs_h, sig_h, idx_ref, own_ref, sch_ref,
-                 sp, cr, r_out, q_out, sums_out,
-                 rhs_v, d_v, fp, rb, blocks, idx_v, own_v, p_v, row_s, row_r, col_s, col_r, sum_buf,
-                 in_sem, small_sem, hs_sem, hr_sem, ag_r, ss_z, ss_y, ss_x, ss_c, sum_s, sum_r):
+def front_kernel(nsx, nsy, rhs_h, sig_h, sch_ref, sp, cr, blocks,
+                 rhs_v, d_v, fp, row_s, row_r, col_s, col_r,
+                 in_sem, small_sem, hs_sem, hr_sem, ag_r, ss_z, ss_y, ss_x, ss_c):
     rows, cols = rhs_v.shape
-    tiles = r_out.shape[0]
     runs = cols // LANES
     nz, nx = nsx // 2, nsy // 2
     n = nsx * nsy
@@ -69,10 +67,8 @@
         pl.semaphore_signal(barrier, inc=1, device_id=(lax.div(o, nsy), lax.rem(o, nsy)),
                             device_id_type=MESH)
 
-    small = [pltpu.make_async_copy(src, dst, small_sem.at[i]) for i, (src, dst) in enumerate((
-        (sch_ref, blocks.at[c, (2 * z + y) * nx + x]), (idx_ref, idx_v), (own_ref, own_v)))]
-    for cp in small:
-        cp.start()
+    own = pltpu.make_async_copy(sch_ref, blocks.at[c, (2 * z + y) * nx + x], small_sem)
+    own.start()
 
     half = LANES // 2
 
@@ -217,8 +213,7 @@
         for cp in loads[i]:
             cp.wait()
         do_first(*regions[i], 32 if i < 2 else 16)
-    for cp in small:
-        cp.wait()
+    own.wait()
     pl.semaphore_wait(barrier, n - 1)
     for h in range(2):
         for i in range(1, nz):
@@ -245,6 +240,47 @@
     for i in range(nz):
         ag_third(i)
 
+    halo_take(1, sp, cps1)
+
+    def rim(row, col, nrows, width):
+        return ((1.0 - CC) * rhs_v[pl.ds(row, nrows), col : col + width]
+                - W2 * halo_sum(fp, row, col, nrows, width) + halo_sum(sp, row, col, nrows, width))
+
+    def put(at, nrows, value):
+        cr[pl.ds(at, nrows), :] = value
+
+    @pl.loop(0, rows // 32)
+    def _(t):
+        r = pl.multiple_of(t * 32, 32)
+        one = rim(r, 0, 32, LANES)
+        two = rim(r, cols - LANES, 32, LANES)
+        put(r, 32, one)
+        put(r + rows, 32, two)
+
+    cr[2 * rows :, :] = jnp.zeros((cr.shape[0] - 2 * rows, LANES), F32)
+    top = rim(0, 0, 1, cols)
+    bottom = rim(rows - 1, 0, 1, cols)
+    for k in range(runs):
+        put(2 * rows + k, 1, top[:, LANES * k : LANES * k + LANES])
+        put(2 * rows + runs + k, 1, bottom[:, LANES * k : LANES * k + LANES])
+
+    do_second(8, rows - 8, LANES, cols - LANES, 16)
+    ag_last()
+    for cp in cps0 + cps1:
+        cp.wait_send()
+    for cp in sends:
+        cp.wait_send()
+
+
+def product_kernel(rows, runs, idx_ref, own_ref, rim_ref, blocks, r_out, q_out, part_out, count_out, rb, p_v, idx_v, own_v, sem):
+    tiles = r_out.shape[0]
+    pair = [pltpu.make_async_copy(a, b, sem.at[i])
+            for i, (a, b) in enumerate(((idx_ref, idx_v), (own_ref, own_v)))]
+    for cp in pair:
+        cp.start()
+    for cp in pair:
+        cp.wait()
+
     index = idx_v[...]
     owner = own_v[...]
     trow = lax.div(index, runs)
@@ -260,36 +296,12 @@
                             + [jnp.zeros((LANES - 4 * nblk, LANES), F32)], axis=0)
     numbers = stack.T
 
-    halo_take(1, sp, cps1)
-
-    def rim(row, col, nrows, width):
-        return ((1.0 - CC) * rhs_v[pl.ds(row, nrows), col : col + width]
-                - W2 * halo_sum(fp, row, col, nrows, width) + halo_sum(sp, row, col, nrows, width))
-
-    def put(at, nrows, value):
-        cr[pl.ds(at, nrows), :] = value
-
-    @pl.loop(0, rows // 32)
-    def _(t):
-        r = pl.multiple_of(t * 32, 32)
-        one = rim(r, 0, 32, LANES)
-        two = rim(r, cols - LANES, 32, LANES)
-        put(r, 32, one)
-        put(r + rows, 32, two)
-
-    cr[2 * rows :, :] = jnp.zeros((cr.shape[0] - 2 * rows, LANES), F32)
-    top = rim(0, 0, 1, cols)
-    bottom = rim(rows - 1, 0, 1, cols)
-    for k in range(runs):
-        put(2 * rows + k, 1, top[:, LANES * k : LANES * k + LANES])
-        put(2 * rows + runs + k, 1, bottom[:, LANES * k : LANES * k + LANES])
-
-    nk = cr.shape[0] // LANES
+    nk = rim_ref.shape[0] // LANES
 
     @pl.loop(0, nk)
     def _(t):
         at = pl.multiple_of(t * LANES, LANES)
-        v = cr[pl.ds(at, LANES), :]
+        v = rim_ref[pl.ds(at, LANES), :]
         hi = v.astype(BF16)
         rb[pl.ds(at, LANES), 0:LANES] = hi
         rb[pl.ds(at, LANES), LANES:] = (v - hi.astype(F32)).astype(BF16)
@@ -326,7 +338,6 @@
         r_out[at : at + m * LANES, :] = r
         rr += fold(r * r)
 
-    ag_last()
     for g in range(nblk // m):
         at = g * m * LANES
         p = p_v[at : at + m * LANES, :]
@@ -335,26 +346,39 @@
 
         def pairs(k0, acc):
             masked = jnp.concatenate(
-                [jnp.where(p16 == (k0 + k if isinstance(k0, int) else (k0 + k).astype(BF16)), p, zero_b)
+                [jnp.where(p16 == k0 + k, p, zero_b)
                  for k in range(gp)], axis=1)
             mats = jnp.concatenate([blocks[0, pl.ds(k0, gp)].reshape(gp * LANES, LANES),
                                     blocks[1, pl.ds(k0, gp)].reshape(gp * LANES, LANES)], axis=1)
             return acc + jnp.dot(masked, mats, preferred_element_type=F32)
 
         acc = jnp.zeros((m * LANES, 2 * LANES), F32)
-        if npair == gp:
-            acc = pairs(0, acc)
-        else:
-            acc = lax.fori_loop(0, npair // gp, lambda s, v: pairs(s * gp, v), acc)
+        for k0 in range(0, npair, gp):
+            acc = pairs(k0, acc)
         qb = jnp.where(spread(3, g) > 0.5, acc[:, LANES:], acc[:, :LANES]).astype(BF16)
         q_out[at : at + m * LANES, :] = qb
         q = qb.astype(F32)
         pq += fold(r * q)
         qq += fold(q * q)
 
-    part = jnp.concatenate([jnp.sum(v, axis=0, keepdims=True) for v in (rr, pq, qq)]
-                           + [jnp.zeros((5, LANES), F32)], axis=0)
-    sum_buf[me] = part
+    part_out[...] = jnp.concatenate([jnp.sum(v, axis=0, keepdims=True) for v in (rr, pq, qq)]
+                                    + [jnp.zeros((5, LANES), F32)], axis=0)
+    count_out[...] = count
+
+
+def sum_kernel(nsx, nsy, part, rim_ref, count, cr, sums_out, sum_buf, sum_s, sum_r):
+    n = nsx * nsy
+    me = lax.axis_index("sx") * nsy + lax.axis_index("sy")
+    barrier = pltpu.get_barrier_semaphore()
+
+    @pl.loop(1, n)
+    def _(k):
+        o = lax.rem(me + k, n)
+        pl.semaphore_signal(barrier, inc=1, device_id=(lax.div(o, nsy), lax.rem(o, nsy)),
+                            device_id_type=MESH)
+
+    sum_buf[me] = part[...]
+    pl.semaphore_wait(barrier, n - 1)
 
     def sum_copy(slot, k):
         o = lax.rem(me + k, n)
@@ -366,15 +390,9 @@
     def _(k):
         sum_copy(me, k).start()
 
-    do_second(8, rows - 8, LANES, cols - LANES, 16)
-    for a in range(nk):
+    for a in range(cr.shape[0] // LANES):
         at = a * LANES
-        cr[at : at + LANES, :] = cr[at : at + LANES, :] * count[:, a : a + 1]
-
-    for cp in cps0 + cps1:
-        cp.wait_send()
-    for cp in sends:
-        cp.wait_send()
+        cr[at : at + LANES, :] = rim_ref[at : at + LANES, :] * count[:, a : a + 1]
 
     @pl.loop(1, n)
     def _(k):
@@ -454,29 +472,48 @@
     dma = pltpu.SemaphoreType.DMA
     padded = (rows + 16, cols + 2 * LANES)
     kept = pltpu.VMEM
-    sp, cr, r, q, sums = pl.pallas_call(
+
+    def in_hbm(v):
+        return pltpu.with_memory_space_constraint(v, pltpu.HBM)
+
+    sp, rim, blocks = pl.pallas_call(
         functools.partial(front_kernel, nsx, nsy),
-        out_shape=[kept(padded, F32), kept((nk * LANES, LANES), F32), kept((tiles, LANES), F32),
-                   kept((tiles, LANES), BF16), kept((8, LANES), F32)],
-        in_specs=[big] * 5,
-        out_specs=[vm] * 5,
+        out_shape=[kept(padded, F32), kept((nk * LANES, LANES), F32), kept((2, n // 2, LANES, LANES), BF16)],
+        in_specs=[big] * 3,
+        out_specs=[vm] * 3,
         scratch_shapes=[
             pltpu.VMEM((rows, cols), F32), pltpu.VMEM((rows, cols), F32), pltpu.VMEM(padded, F32),
-            pltpu.VMEM((nk * LANES, 2 * LANES), BF16), pltpu.VMEM((2, n // 2, LANES, LANES), BF16),
-            pltpu.VMEM((tiles // LANES, LANES), jnp.int32), pltpu.VMEM((tiles // LANES, LANES), jnp.int32),
-            pltpu.VMEM((tiles, LANES), BF16),
             pltpu.VMEM((2, 2, 1, cols), F32), pltpu.VMEM((2, 2, 1, cols), F32),
             pltpu.VMEM((2, 2, 8, LANES), F32), pltpu.VMEM((2, 2, 8, LANES), F32),
-            pltpu.VMEM((n, 8, LANES), F32),
-            dma((2, 8)), dma((3,)), dma((2, 4)), dma((2, 4)), dma((2, n)), dma((2, nz)), dma((2, nz, nx)),
-            dma((2, nz, 2, nx)), dma((2, nz, 2, nx)), dma((n,)), dma((n,)),
+            dma((2, 8)), dma, dma((2, 4)), dma((2, 4)), dma((2, n)), dma((2, nz)), dma((2, nz, nx)),
+            dma((2, nz, 2, nx)), dma((2, nz, 2, nx)),
         ],
         compiler_params=pltpu.CompilerParams(
-            collective_id=0, has_side_effects=True, vmem_limit_bytes=44 * 2**20),
+            collective_id=0, has_side_effects=True, vmem_limit_bytes=32 * 2**20),
         name="front",
-    )(*[pltpu.with_memory_space_constraint(v, pltpu.HBM) for v in (
-        rhs, sigma, tile_list.reshape(-1, LANES), tile_owner.reshape(-1, LANES),
-        schur_blocks.reshape(LANES, LANES))])
+    )(in_hbm(rhs), in_hbm(sigma), in_hbm(schur_blocks.reshape(LANES, LANES)))
+    r, q, part, count = pl.pallas_call(
+        functools.partial(product_kernel, rows, cols // LANES),
+        out_shape=[kept((tiles, LANES), F32), kept((tiles, LANES), BF16), kept((8, LANES), F32),
+                   kept((LANES, LANES), F32)],
+        in_specs=[big, big, vm, vm],
+        out_specs=[vm] * 4,
+        scratch_shapes=[pltpu.VMEM((nk * LANES, 2 * LANES), BF16), pltpu.VMEM((tiles, LANES), BF16),
+                        pltpu.VMEM((tiles // LANES, LANES), jnp.int32),
+                        pltpu.VMEM((tiles // LANES, LANES), jnp.int32), dma((2,))],
+        compiler_params=pltpu.CompilerParams(vmem_limit_bytes=24 * 2**20),
+        name="products",
+    )(in_hbm(tile_list.reshape(-1, LANES)), in_hbm(tile_owner.reshape(-1, LANES)), rim, blocks)
+    cr, sums = pl.pallas_call(
+        functools.partial(sum_kernel, nsx, nsy),
+        out_shape=[kept((nk * LANES, LANES), F32), kept((8, LANES), F32)],
+        in_specs=[vm] * 3,
+        out_specs=[vm] * 2,
+        scratch_shapes=[pltpu.VMEM((n, 8, LANES), F32), dma((n,)), dma((n,))],
+        compiler_params=pltpu.CompilerParams(
+            collective_id=1, has_side_effects=True, vmem_limit_bytes=4 * 2**20),
+        name="sums",
+    )(part, rim, count)
     nch = 4
     return pl.pallas_call(
         back_kernel,

time: 46.7 us -> 53.9 us (1.15)
  Pallas kernels: 45.9 us -> 53 us
    pallas_call x0 -> x2, Pallas kernels: none -> 14.1 us  [the longest x1 8.28 us: per_device(): pl.pallas_call(functools.partial(sum_kernel, nsx, nsy), out_shape=[kept((...]
    pallas_call x1, Pallas kernels: 42.5 us -> 35.5 us  [per_device(): pl.pallas_call(functools.partial(front_kernel, nsx, nsy), out_shape=[kept...]
where the time goes in v3:
time: 53.9 us; the launch traced here: 53.7 us
  Pallas kernels  53 us (98%)
  between operations  0.65 us (1%)
    pallas_call x1, Pallas kernels, per_device(): pl.pallas_call(functools.partial(front_kernel, nsx, nsy), out_shape=[kept...  35.5 us
    pallas_call x1, Pallas kernels, per_device(): pl.pallas_call(functools.partial(sum_kernel, nsx, nsy), out_shape=[kept((...  8.28 us
    pallas_call x1, Pallas kernels, per_device(): pl.pallas_call(functools.partial(product_kernel, rows, cols // LANES), ou...  5.87 us
    pallas_call x1, Pallas kernels, per_device(): pl.pallas_call(back_kernel, out_shape=[jax.ShapeDtypeStruct((rows, cols),...  3.4 us

profile of v3, /device:TPU:0, one launch (start us, length us, event | category | flops | bytes accessed | tf_op | source)
XLA Modules:
  0.0 53.7 jit_solution(3183064902870810431)
XLA Ops:
  0.6 35.5 %front.1 = (f32[784,2304]{1,0:T(8,128)S(1)}, f32[1664,128]{1,0:T(8,128)S(1)}, bf16[2,16,128,128]{3,2,1,0:T(8,128)(2,1)S(1)}) custom-call(f32[768,2048]{1,0:T(8,128)} %rhs_h.1, f32[768,2048]{1,0:T(8,128)} %sig_h.1, bf16[128,128]{1,0:T(8,128)(2,1)} %bitcast.3), custom_call_target="tpu_custom_call" | custom-call | tf_op jit(solution)/shard_map/front/pallas_call | solution.py:479
  36.1 5.9 %products.1 = (f32[2048,128]{1,0:T(8,128)S(1)}, bf16[2048,128]{1,0:T(8,128)(2,1)S(1)}, f32[8,128]{1,0:T(8,128)S(1)}, f32[128,128]{1,0:T(8,128)S(1)}) custom-call(s32[16,128]{1,0:T(8,128)} %bitcast.4, s32[16,128]{1,0:T(8,128)} %bitcast.5, f32[1664,128]{1,0:T(8,128)S(1)} %get-tuple-element.13.rim_ref, bf16[2,16,128,128]{3,2,1,0:T(8,128)(2,1)S(1)} %get-tuple-element.14.blocks), custom_call_target="tpu_custom_call" | custom-call | tf_op jit(solution)/shard_map/products/pallas_call | solution.py:495
  42.0 8.3 %sums.1 = (f32[1664,128]{1,0:T(8,128)S(1)}, f32[8,128]{1,0:T(8,128)S(1)}) custom-call(f32[8,128]{1,0:T(8,128)S(1)} %get-tuple-element.15.part, f32[1664,128]{1,0:T(8,128)S(1)} %get-tuple-element.13.rim_ref, f32[128,128]{1,0:T(8,128)S(1)} %get-tuple-element.16.count), custom_call_target="tpu_custom_call" | custom-call | tf_op jit(solution)/shard_map/sums/pallas_call | solution.py:507
  50.3 3.4 %back.1 = (f32[768,2048]{1,0:T(8,128)}, f32[2048,128]{1,0:T(8,128)}, f32[2048,128]{1,0:T(8,128)}) custom-call(f32[784,2304]{1,0:T(8,128)S(1)} %get-tuple-element.12.sp, f32[1664,128]{1,0:T(8,128)S(1)} %get-tuple-element.17.cr, f32[2048,128]{1,0:T(8,128)S(1)} %get-tuple-element.18.r_ref, bf16[2048,128]{1,0:T(8,128)(2,1)S(1)} %get-tuple-element.19.q_ref, ...), custom_call_target="tpu_custom_call" | custom-call | tf_op jit(solution)/shard_map/back/pallas_call | solution.py:518

commit v4 on v3

--- a/solution.py
+++ b/solution.py
@@ -29,18 +29,13 @@
     return (left + right) + (up + down)
 
 
-def front_kernel(nsx, nsy, rhs_h, sig_h, sch_ref, sp, cr, blocks,
+def front_kernel(nsx, nsy, rhs_h, sig_h, sp, cr,
                  rhs_v, d_v, fp, row_s, row_r, col_s, col_r,
-                 in_sem, small_sem, hs_sem, hr_sem, ag_r, ss_z, ss_y, ss_x, ss_c):
+                 in_sem, hs_sem, hr_sem):
     rows, cols = rhs_v.shape
     runs = cols // LANES
-    nz, nx = nsx // 2, nsy // 2
-    n = nsx * nsy
     sx = lax.axis_index("sx")
     sy = lax.axis_index("sy")
-    me = sx * nsy + sy
-    z, y = lax.div(sx, 2), lax.rem(sx, 2)
-    x, c = lax.div(sy, 2), lax.rem(sy, 2)
 
     left, right = (0, 2 * LANES), (cols - 2 * LANES, cols)
     regions = [(0, rows) + left, (0, rows) + right,
@@ -59,83 +54,6 @@
             pair.append(cp)
         loads.append(pair)
 
-    barrier = pltpu.get_barrier_semaphore()
-
-    @pl.loop(1, n)
-    def _(k):
-        o = lax.rem(me + k, n)
-        pl.semaphore_signal(barrier, inc=1, device_id=(lax.div(o, nsy), lax.rem(o, nsy)),
-                            device_id_type=MESH)
-
-    own = pltpu.make_async_copy(sch_ref, blocks.at[c, (2 * z + y) * nx + x], small_sem)
-    own.start()
-
-    half = LANES // 2
-
-    def piece(h, zz, yy, xx, cc, dev, sem):
-        pair = (2 * zz + yy) * nx + xx
-        ref = blocks.at[cc, pair, pl.ds(h * half, half), :]
-        dz, dy, dx, dc = dev
-        return pltpu.make_async_remote_copy(
-            ref, ref, sem, ag_r.at[h, 2 * pair + cc],
-            device_id=(2 * dz + dy, 2 * dx + dc), device_id_type=MESH)
-
-    sends = []
-
-    def send(*args):
-        cp = piece(*args)
-        cp.start()
-        sends.append(cp)
-
-    def arrived(h, zz, yy, xx, cc):
-        piece(h, zz, yy, xx, cc, (z, y, x, 1 - c), ss_c.at[0, 0, 0, 0]).wait_recv()
-
-    zs = [lax.rem(z + k, nz) for k in range(nz)]
-    ys = [y, 1 - y]
-    xs = [lax.rem(x + k, nx) for k in range(nx)]
-
-    def to_core(h, i, j, k):
-        send(h, zs[i], ys[j], xs[k], c, (z, y, x, 1 - c), ss_c.at[h, i, j, k])
-
-    def ag_first(i):
-        for h in range(2):
-            if i:
-                arrived(h, zs[i], y, x, c)
-            if h == 0:
-                send(0, zs[i], y, x, c, (z, 1 - y, x, c), ss_y.at[0, i, 0])
-            for k in range(1, nx):
-                send(h, zs[i], y, x, c, (z, y, xs[k], c), ss_x.at[h, i, 0, k])
-            if h == 1:
-                send(1, zs[i], y, x, c, (z, 1 - y, x, c), ss_y.at[1, i, 0])
-            to_core(h, i, 0, 0)
-
-    def ag_second(i):
-        arrived(0, zs[i], 1 - y, x, c)
-        for k in range(1, nx):
-            send(0, zs[i], 1 - y, x, c, (z, y, xs[k], c), ss_x.at[0, i, 1, k])
-        to_core(0, i, 1, 0)
-        for k in range(1, nx):
-            arrived(1, zs[i], y, xs[k], c)
-            send(1, zs[i], y, xs[k], c, (z, 1 - y, x, c), ss_y.at[1, i, k])
-            to_core(1, i, 0, k)
-
-    def ag_third(i):
-        for k in range(1, nx):
-            arrived(0, zs[i], y, xs[k], c)
-            to_core(0, i, 0, k)
-            arrived(0, zs[i], 1 - y, xs[k], c)
-            to_core(0, i, 1, k)
-        for k in range(nx):
-            arrived(1, zs[i], 1 - y, xs[k], c)
-            to_core(1, i, 1, k)
-
-    def ag_last():
-        for h in range(2):
-            for i in range(nz):
-                for j in range(2):
-                    for k in range(nx):
-                        arrived(h, zs[i], ys[j], xs[k], 1 - c)
-
     def do_first(r0, r1, c0, c1, b):
         w = c1 - c0
 
@@ -165,6 +83,10 @@
     down_dev = (lax.rem(sx + 1, nsx), sy)
     left_dev = (sx, lax.rem(sy + nsy - 1, nsy))
     right_dev = (sx, lax.rem(sy + 1, nsy))
+
+    barrier = pltpu.get_barrier_semaphore()
+    for dev in (up_dev, down_dev, left_dev, right_dev):
+        pl.semaphore_signal(barrier, inc=1, device_id=dev, device_id_type=MESH)
 
     def halo_copies(ph):
         out = []
@@ -213,32 +135,19 @@
         for cp in loads[i]:
             cp.wait()
         do_first(*regions[i], 32 if i < 2 else 16)
-    own.wait()
-    pl.semaphore_wait(barrier, n - 1)
-    for h in range(2):
-        for i in range(1, nz):
-            send(h, z, y, x, c, (zs[i], y, x, c), ss_z.at[h, i])
+    pl.semaphore_wait(barrier, 4)
     cps0 = halo_send(0, fp)
-    ag_first(0)
-    for cp in loads[4]:
-        cp.wait()
-    do_first(*regions[4], 16)
-    for i in range(1, nz):
-        ag_first(i)
+    for i in range(4, 4 + chunks):
+        for cp in loads[i]:
+            cp.wait()
+        do_first(*regions[i], 16)
     halo_take(0, fp, cps0)
     do_second(0, rows, *left, 32)
     do_second(0, rows, *right, 32)
     do_second(0, 8, LANES, cols - LANES, 8)
     do_second(rows - 8, rows, LANES, cols - LANES, 8)
     cps1 = halo_send(1, sp)
-    for i in range(nz):
-        ag_second(i)
-    for i in range(5, 4 + chunks):
-        for cp in loads[i]:
-            cp.wait()
-        do_first(*regions[i], 16)
-    for i in range(nz):
-        ag_third(i)
+    do_second(8, rows - 8, LANES, cols - LANES, 16)
 
     halo_take(1, sp, cps1)
 
@@ -264,20 +173,26 @@
         put(2 * rows + k, 1, top[:, LANES * k : LANES * k + LANES])
         put(2 * rows + runs + k, 1, bottom[:, LANES * k : LANES * k + LANES])
 
-    do_second(8, rows - 8, LANES, cols - LANES, 16)
-    ag_last()
     for cp in cps0 + cps1:
         cp.wait_send()
-    for cp in sends:
-        cp.wait_send()
-
-
-def product_kernel(rows, runs, idx_ref, own_ref, rim_ref, blocks, r_out, q_out, part_out, count_out, rb, p_v, idx_v, own_v, sem):
+
+
+def product_kernel(nsx, nsy, rows, runs, idx_ref, own_ref, blocks_h, rim_ref, cr, r_out, q_out, sums_out,
+                   rb, p_v, idx_v, own_v, blocks, one_buf, two_buf, sem, one_s, one_r, two_s, two_r):
+    sx = lax.axis_index("sx")
+    sy = lax.axis_index("sy")
+    barrier = pltpu.get_barrier_semaphore()
+    for k in range(1, nsy):
+        pl.semaphore_signal(barrier, inc=1, device_id=(sx, lax.rem(sy + k, nsy)), device_id_type=MESH)
+    for k in range(1, nsx):
+        pl.semaphore_signal(barrier, inc=1, device_id=(lax.rem(sx + k, nsx), sy), device_id_type=MESH)
     tiles = r_out.shape[0]
     pair = [pltpu.make_async_copy(a, b, sem.at[i])
             for i, (a, b) in enumerate(((idx_ref, idx_v), (own_ref, own_v)))]
+    fetch = pltpu.make_async_copy(blocks_h, blocks, sem.at[2])
     for cp in pair:
         cp.start()
+    fetch.start()
     for cp in pair:
         cp.wait()
 
@@ -322,7 +237,7 @@
     def fold(v):
         return jnp.sum(v.reshape(-1, 8, LANES), axis=0)
 
-    npair = blocks.shape[1]
+    npair = blocks.shape[0] // 2
     gp = min(npair, 16)
     for g in range(nblk // m):
         at = g * m * LANES
@@ -338,6 +253,7 @@
         r_out[at : at + m * LANES, :] = r
         rr += fold(r * r)
 
+    fetch.wait()
     for g in range(nblk // m):
         at = g * m * LANES
         p = p_v[at : at + m * LANES, :]
@@ -348,8 +264,9 @@
             masked = jnp.concatenate(
                 [jnp.where(p16 == k0 + k, p, zero_b)
                  for k in range(gp)], axis=1)
-            mats = jnp.concatenate([blocks[0, pl.ds(k0, gp)].reshape(gp * LANES, LANES),
-                                    blocks[1, pl.ds(k0, gp)].reshape(gp * LANES, LANES)], axis=1)
+            mats = jnp.concatenate(
+                [jnp.concatenate([blocks[2 * (k0 + k)], blocks[2 * (k0 + k) + 1]], axis=1)
+                 for k in range(gp)], axis=0)
             return acc + jnp.dot(masked, mats, preferred_element_type=F32)
 
         acc = jnp.zeros((m * LANES, 2 * LANES), F32)
@@ -361,45 +278,39 @@
         pq += fold(r * q)
         qq += fold(q * q)
 
-    part_out[...] = jnp.concatenate([jnp.sum(v, axis=0, keepdims=True) for v in (rr, pq, qq)]
-                                    + [jnp.zeros((5, LANES), F32)], axis=0)
-    count_out[...] = count
-
-
-def sum_kernel(nsx, nsy, part, rim_ref, count, cr, sums_out, sum_buf, sum_s, sum_r):
-    n = nsx * nsy
-    me = lax.axis_index("sx") * nsy + lax.axis_index("sy")
-    barrier = pltpu.get_barrier_semaphore()
-
-    @pl.loop(1, n)
-    def _(k):
-        o = lax.rem(me + k, n)
-        pl.semaphore_signal(barrier, inc=1, device_id=(lax.div(o, nsy), lax.rem(o, nsy)),
-                            device_id_type=MESH)
-
-    sum_buf[me] = part[...]
-    pl.semaphore_wait(barrier, n - 1)
-
-    def sum_copy(slot, k):
-        o = lax.rem(me + k, n)
+    def one_copy(slot, k):
         return pltpu.make_async_remote_copy(
-            sum_buf.at[slot], sum_buf.at[slot], sum_s.at[k], sum_r.at[slot],
-            device_id=(lax.div(o, nsy), lax.rem(o, nsy)), device_id_type=MESH)
-
-    @pl.loop(1, n)
-    def _(k):
-        sum_copy(me, k).start()
-
-    for a in range(cr.shape[0] // LANES):
+            one_buf.at[slot], one_buf.at[slot], one_s.at[k], one_r.at[slot],
+            device_id=(sx, lax.rem(sy + k, nsy)), device_id_type=MESH)
+
+    def two_copy(slot, k):
+        return pltpu.make_async_remote_copy(
+            two_buf.at[slot], two_buf.at[slot], two_s.at[k], two_r.at[slot],
+            device_id=(lax.rem(sx + k, nsx), sy), device_id_type=MESH)
+
+    one_buf[sy] = jnp.concatenate([jnp.sum(v, axis=0, keepdims=True) for v in (rr, pq, qq)]
+                                  + [jnp.zeros((5, LANES), F32)], axis=0)
+    pl.semaphore_wait(barrier, nsx + nsy - 2)
+    for k in range(1, nsy):
+        one_copy(sy, k).start()
+    for a in range(nk // 2):
         at = a * LANES
         cr[at : at + LANES, :] = rim_ref[at : at + LANES, :] * count[:, a : a + 1]
-
-    @pl.loop(1, n)
-    def _(k):
-        sum_copy(me, k).wait_send()
-        sum_copy(lax.rem(me + k, n), k).wait_recv()
-
-    sums_out[...] = jnp.sum(sum_buf[...], axis=0)
+    for k in range(1, nsy):
+        one_copy(lax.rem(sy + k, nsy), k).wait_recv()
+    two_buf[sx] = jnp.sum(one_buf[...], axis=0)
+    for k in range(1, nsx):
+        two_copy(sx, k).start()
+    for a in range(nk // 2, nk):
+        at = a * LANES
+        cr[at : at + LANES, :] = rim_ref[at : at + LANES, :] * count[:, a : a + 1]
+    for k in range(1, nsx):
+        two_copy(lax.rem(sx + k, nsx), k).wait_recv()
+    sums_out[...] = jnp.sum(two_buf[...], axis=0)
+    for k in range(1, nsy):
+        one_copy(sy, k).wait_send()
+    for k in range(1, nsx):
+        two_copy(sx, k).wait_send()
 
 
 def back_kernel(sp, cr, r_ref, q_ref, sums, out, res, direc,
@@ -463,8 +374,6 @@
 def per_device(nsx, nsy, rhs, sigma, tile_list, tile_owner, schur_blocks):
     rows, cols = rhs.shape
     tiles = tile_list.shape[0]
-    n = nsx * nsy
-    nz, nx = nsx // 2, nsy // 2
     nk = -(-(2 * rows + 2 * (cols // LANES)) // LANES)
     vm = pl.BlockSpec(memory_space=pltpu.VMEM)
     hbm = pl.BlockSpec(memory_space=pl.ANY)
@@ -476,44 +385,40 @@
     def in_hbm(v):
         return pltpu.with_memory_space_constraint(v, pltpu.HBM)
 
-    sp, rim, blocks = pl.pallas_call(
+    blocks = lax.all_gather(schur_blocks, ("sx", "sy"), axis=0, tiled=True)
+    sp, rim = pl.pallas_call(
         functools.partial(front_kernel, nsx, nsy),
-        out_shape=[kept(padded, F32), kept((nk * LANES, LANES), F32), kept((2, n // 2, LANES, LANES), BF16)],
-        in_specs=[big] * 3,
-        out_specs=[vm] * 3,
+        out_shape=[kept(padded, F32), kept((nk * LANES, LANES), F32)],
+        in_specs=[big] * 2,
+        out_specs=[vm] * 2,
         scratch_shapes=[
             pltpu.VMEM((rows, cols), F32), pltpu.VMEM((rows, cols), F32), pltpu.VMEM(padded, F32),
             pltpu.VMEM((2, 2, 1, cols), F32), pltpu.VMEM((2, 2, 1, cols), F32),
             pltpu.VMEM((2, 2, 8, LANES), F32), pltpu.VMEM((2, 2, 8, LANES), F32),
-            dma((2, 8)), dma, dma((2, 4)), dma((2, 4)), dma((2, n)), dma((2, nz)), dma((2, nz, nx)),
-            dma((2, nz, 2, nx)), dma((2, nz, 2, nx)),
+            dma((2, 8)), dma((2, 4)), dma((2, 4)),
         ],
         compiler_params=pltpu.CompilerParams(
             collective_id=0, has_side_effects=True, vmem_limit_bytes=32 * 2**20),
+        cost_estimate=pl.CostEstimate(flops=40 * rows * cols, bytes_accessed=12 * rows * cols,
+                                      transcendentals=0),
         name="front",
-    )(in_hbm(rhs), in_hbm(sigma), in_hbm(schur_blocks.reshape(LANES, LANES)))
-    r, q, part, count = pl.pallas_call(
-        functools.partial(product_kernel, rows, cols // LANES),
-        out_shape=[kept((tiles, LANES), F32), kept((tiles, LANES), BF16), kept((8, LANES), F32),
-                   kept((LANES, LANES), F32)],
-        in_specs=[big, big, vm, vm],
+    )(in_hbm(rhs), in_hbm(sigma))
+    cr, r, q, sums = pl.pallas_call(
+        functools.partial(product_kernel, nsx, nsy, rows, cols // LANES),
+        out_shape=[kept((nk * LANES, LANES), F32), kept((tiles, LANES), F32), kept((tiles, LANES), BF16),
+                   kept((8, LANES), F32)],
+        in_specs=[big, big, big, vm],
         out_specs=[vm] * 4,
         scratch_shapes=[pltpu.VMEM((nk * LANES, 2 * LANES), BF16), pltpu.VMEM((tiles, LANES), BF16),
                         pltpu.VMEM((tiles // LANES, LANES), jnp.int32),
-                        pltpu.VMEM((tiles // LANES, LANES), jnp.int32), dma((2,))],
-        compiler_params=pltpu.CompilerParams(vmem_limit_bytes=24 * 2**20),
+                        pltpu.VMEM((tiles // LANES, LANES), jnp.int32),
+                        pltpu.VMEM((nsx * nsy, LANES, LANES), BF16),
+                        pltpu.VMEM((nsy, 8, LANES), F32), pltpu.VMEM((nsx, 8, LANES), F32), dma((3,)),
+                        dma((nsy,)), dma((nsy,)), dma((nsx,)), dma((nsx,))],
+        compiler_params=pltpu.CompilerParams(
+            collective_id=1, has_side_effects=True, vmem_limit_bytes=24 * 2**20),
         name="products",
-    )(in_hbm(tile_list.reshape(-1, LANES)), in_hbm(tile_owner.reshape(-1, LANES)), rim, blocks)
-    cr, sums = pl.pallas_call(
-        functools.partial(sum_kernel, nsx, nsy),
-        out_shape=[kept((nk * LANES, LANES), F32), kept((8, LANES), F32)],
-        in_specs=[vm] * 3,
-        out_specs=[vm] * 2,
-        scratch_shapes=[pltpu.VMEM((n, 8, LANES), F32), dma((n,)), dma((n,))],
-        compiler_params=pltpu.CompilerParams(
-            collective_id=1, has_side_effects=True, vmem_limit_bytes=4 * 2**20),
-        name="sums",
-    )(part, rim, count)
+    )(in_hbm(tile_list.reshape(-1, LANES)), in_hbm(tile_owner.reshape(-1, LANES)), in_hbm(blocks), rim)
     nch = 4
     return pl.pallas_call(
         back_kernel,

time: 53.9 us -> 94 us (1.74)
  waiting for transfers between devices: 0 us -> 30.3 us
  between operations: 0.65 us -> 14.1 us
  Pallas kernels: 53 us -> 43.4 us
  local copies, waits for them, and re-layouts: 0 us -> 5.97 us
    all_gather x0 -> x1, waiting for transfers between devices: none -> 29.6 us  [per_device(): blocks = lax.all_gather(schur_blocks, ('sx', 'sy'), axis=0, tiled=True)]
    pallas_call x1, Pallas kernels: 35.5 us -> 26.8 us  [per_device(): pl.pallas_call(functools.partial(front_kernel, nsx, nsy), out_shape=[kept...]
    unnamed x0 -> x4, local copies, waits for them, and re-layouts: none -> 5.97 us
    pallas_call x2 -> x1, Pallas kernels: 14.1 us -> 13.3 us  [per_device(): pl.pallas_call(functools.partial(product_kernel, nsx, nsy, rows, cols //...]
  transfers between devices with their start and end apart: 0 -> 1, of which waited for: 0 -> 1; matrix products, arithmetic and copies ran while one was open for 0% -> 0% of each run, Pallas kernels for 0% -> 29%
where the time goes in v4:
time: 94 us; the launch traced here: 93.8 us
  Pallas kernels  43.4 us (46%)
  waiting for transfers between devices  30.3 us (32%)
  between operations  14.1 us (15%)
  local copies, waits for them, and re-layouts  5.97 us (6%)
    all_gather x1, waiting for transfers between devices, per_device(): blocks = lax.all_gather(schur_blocks, ('sx', 'sy'), axis=0, tiled=True)  29.6 us
    pallas_call x1, Pallas kernels, per_device(): pl.pallas_call(functools.partial(front_kernel, nsx, nsy), out_shape=[kept...  26.8 us
    pallas_call x1, Pallas kernels, per_device(): pl.pallas_call(functools.partial(product_kernel, nsx, nsy, rows, cols //...  13.3 us
    unnamed x4, local copies, waits for them, and re-layouts  5.97 us
    pallas_call x1, Pallas kernels, per_device(): pl.pallas_call(back_kernel, out_shape=[jax.ShapeDtypeStruct((rows, cols),...  3.39 us
  transfers between devices with their start and end apart: 1, of which 1 were waited for; matrix products, arithmetic and copies ran while one was open for 0% of the time, Pallas kernels for 29%

profile of v4, /device:TPU:0, one launch (start us, length us, event | category | flops | bytes accessed | tf_op | source)
XLA Modules:
  0.0 93.8 jit_solution(1264030871847781517)
XLA Ops:
  7.2 0.0 all-gather.2.cloned.1.call-start
  7.2 0.7 all-gather.2.cloned.1.call-update
  7.9 26.8 %front.1 = (f32[784,2304]{1,0:T(8,128)S(1)}, f32[1664,128]{1,0:T(8,128)S(1)}) custom-call(f32[768,2048]{1,0:T(8,128)} %rhs_h.1, f32[768,2048]{1,0:T(8,128)} %sig_h.1), custom_call_target="tpu_custom_call" | custom-call | flops 62914560 | bytes 18874368 | tf_op jit(solution)/shard_map/front/pallas_call | solution.py:389
  34.7 0.0 copy-start
  34.7 2.9 %copy-done = f32[784,2304]{1,0:T(8,128)} copy-done((f32[784,2304]{1,0:T(8,128)}, f32[784,2304]{1,0:T(8,128)S(1)}, u32[]{:S(2)}) %copy-start) | copy-done | bytes 7225368
  37.6 29.6 %all-gather.2.cloned.1.call-done.blocks_h = bf16[32,128,128]{2,1,0:T(8,128)(2,1)} async-done(((bf16[1,128,128]{2,1,0:T(8,128)(2,1)}), bf16[32,128,128]{2,1,0:T(8,128)(2,1)}) %all-gather.2.cloned.1.call-update) | async-done | bytes 1048592 | tf_op jit(solution)/shard_map/all_gather | solution.py:388
  67.3 13.3 %products.1 = (f32[1664,128]{1,0:T(8,128)S(1)}, f32[2048,128]{1,0:T(8,128)S(1)}, bf16[2048,128]{1,0:T(8,128)(2,1)S(1)}, f32[8,128]{1,0:T(8,128)S(1)}) custom-call(s32[16,128]{1,0:T(8,128)} %bitcast.2, s32[16,128]{1,0:T(8,128)} %bitcast.3, bf16[32,128,128]{2,1,0:T(8,128)(2,1)} %all-gather.2.cloned.1.call-done.blocks_h, f32[1664,128]{1,0:T(8,128)S(1)} %get-tuple-element.10.rim_ref), custom_call_target="tpu_custom_call" | custom-call | tf_op jit(solution)/shard_map/products/pallas_call | solution.py:406
  80.5 0.0 copy-start.1
  80.6 3.0 %copy-done.1 = f32[784,2304]{1,0:T(8,128)S(1)} copy-done((f32[784,2304]{1,0:T(8,128)S(1)}, f32[784,2304]{1,0:T(8,128)}, u32[]{:S(2)}) %copy-start.1) | copy-done | bytes 7225368
  83.6 3.4 %back.1 = (f32[768,2048]{1,0:T(8,128)}, f32[2048,128]{1,0:T(8,128)}, f32[2048,128]{1,0:T(8,128)}) custom-call(f32[784,2304]{1,0:T(8,128)S(1)} %copy-done.1, f32[1664,128]{1,0:T(8,128)S(1)} %get-tuple-element.11.cr, f32[2048,128]{1,0:T(8,128)S(1)} %get-tuple-element.12.r_ref, bf16[2048,128]{1,0:T(8,128)(2,1)S(1)} %get-tuple-element.13.q_ref, ...), custom_call_target="tpu_custom_call" | custom-call | tf_op jit(solution)/shard_map/back/pallas_call | solution.py:423
Async XLA Ops:
  7.2 60.1 %all-gather.2.cloned.1.call-start = ((), (), s32[]{:S(2)}) async-start(), calls=%async_computation | async-start | bytes 1081344 | tf_op jit(solution)/shard_map/all_gather | solution.py:388
  34.7 2.9 %copy-start = (f32[784,2304]{1,0:T(8,128)}, f32[784,2304]{1,0:T(8,128)S(1)}, u32[]{:S(2)}) copy-start(f32[784,2304]{1,0:T(8,128)S(1)} %get-tuple-element.9.sp) | copy-start | bytes 21676036
  80.5 3.1 %copy-start.1 = (f32[784,2304]{1,0:T(8,128)S(1)}, f32[784,2304]{1,0:T(8,128)}, u32[]{:S(2)}) copy-start(f32[784,2304]{1,0:T(8,128)} %copy-done) | copy-start | bytes 21676036
Sparse Core Ops, SparseCore 0:
  10.9 56.3 all-gather.1
